TPU v7x, 512 devices: a whole 4x8x8 slice. The times are simulated.
512 devices in a mesh: group: 8 (over y_lo, core), dp: 64 (over x, y_hi, z).
Axes of the slice: x: 4, y: 8 (y_hi: 2, y_lo: 4; y = y_hi * 4 + y_lo), z: 8, core: 2. Of those that a mesh axis runs over, the one named last changes fastest.
Arguments:
- partials: bfloat16 [8, 64, 2, 384, 1024], P('group', 'dp'), as said below
- momentum: float32 [8, 2, 384, 1024], P('group', None, 'dp'), may hold values from -6 to 6
Outputs:
- update: bfloat16 [8, 2, 384, 1024], P('group')
- momentum_out: float32 [8, 2, 384, 1024], P('group', None, 'dp')
Inputs may be any that keep to these rules, and one draw needn't show every extreme that they name: `partials`: each replica's gradient has row and column scales that differ.
All inputs are finite; a program needn't handle non-finite values.
Results may differ from a plain program's by a relative error of at most 0.023.
Values may be sent and summed in bfloat16 or wider, within the bound.
A program may use at most 64 MiB of HBM per device.

v0:
```python
import math

import jax
import jax.numpy as jnp
from jax import lax
from jax.sharding import PartitionSpec as P

MATS = 2
ROWS = 384
COLS = 1024
ITERS = 5


decay_rate = 0.95
coef_a = 3.4445
coef_b = -4.775
coef_c = 2.0315


def newton_schulz(matrix):
    as_float = matrix.astype(jnp.float32)
    frob_norm = jnp.sqrt(jnp.sum(as_float * as_float))
    current = (as_float / (frob_norm + 1e-07)).astype(jnp.bfloat16)
    final_scale = 0.2 * math.sqrt(max(ROWS, COLS))
    result = None
    for iteration in range(ITERS):
        gram_matrix = jnp.dot(current, current.T, preferred_element_type=jnp.float32).astype(
            jnp.bfloat16
        )
        gram_square = jnp.dot(gram_matrix, gram_matrix, preferred_element_type=jnp.float32)
        mixed_poly = (coef_b * gram_matrix.astype(jnp.float32) + coef_c * gram_square).astype(
            jnp.bfloat16
        )
        stepped = coef_a * current.astype(jnp.float32) + jnp.dot(
            mixed_poly, current, preferred_element_type=jnp.float32
        )
        if iteration + 1 < ITERS:
            current = stepped.astype(jnp.bfloat16)
        else:
            result = (stepped * final_scale).astype(jnp.bfloat16)
    return result


def shards(partials, momentum):
    dp_count = lax.axis_size("dp")
    my_index = lax.axis_index("dp")
    stride = dp_count // MATS
    local_terms = partials[0, 0].astype(jnp.float32)
    summed = lax.psum_scatter(local_terms, "dp", scatter_dimension=1, tiled=True)
    block_rows = summed.shape[1]
    square_sum = lax.psum(jnp.sum(summed * summed), ("group", "dp"))
    entries = lax.axis_size("group") * MATS * ROWS * COLS
    clip_factor = jnp.minimum(1.0, math.sqrt(entries) / jnp.sqrt(square_sum + 1e-06))
    grad = clip_factor * summed
    momentum_out = decay_rate * momentum[0] + grad
    blended = (grad + decay_rate * momentum_out).astype(jnp.bfloat16)
    owners = jnp.arange(MATS, dtype=jnp.int32) * stride
    slot_table = (jnp.arange(dp_count, dtype=jnp.int32)[:, None] == owners[None, :]).astype(
        jnp.bfloat16
    )
    gathered = lax.all_gather(blended, "dp", axis=1, tiled=True)
    own_flags = (owners == my_index).astype(jnp.bfloat16)
    selected = jnp.einsum(
        "m,mrc->rc", own_flags, gathered, preferred_element_type=jnp.float32
    ).astype(jnp.bfloat16)
    result = newton_schulz(selected)
    pieces = lax.all_to_all(
        result.reshape(dp_count, block_rows, COLS), "dp", split_axis=0, concat_axis=0, tiled=True
    )
    row_blocks = jnp.einsum(
        "jm,jrc->mrc", slot_table, pieces, preferred_element_type=jnp.float32
    ).astype(jnp.bfloat16)
    update = lax.all_gather(row_blocks, "dp", axis=1, tiled=True)
    return (update[None], momentum_out[None])


def solution(mesh):
    in_specs = (P("group", "dp", None, None, None), P("group", None, "dp", None))
    out_specs = (P("group", None, None, None), P("group", None, "dp", None))
    return jax.shard_map(shards, mesh=mesh, in_specs=in_specs, out_specs=out_specs, check_vma=False)
```

profile of v0, /device:TPU:1, one launch (start us, length us, event | category | flops | bytes accessed | tf_op | source)
XLA Modules:
  0.0 1275.4 jit_solution(17344022261120984317)
XLA Ops:
  7.2 4.7 bitcast_convert_fusion
  12.0 1.3 dynamic-slice
  13.9 810.0 %all-reduce.3.cloned.1.call-done = f32[2,384,1024]{2,0,1:T(2,128)} async-done(((f32[2,384,1024]{2,0,1:T(2,128)}), f32[2,384,1024]{2,0,1:T(2,128)}) %all-reduce.3.cloned.1.call-update) | async-done | bytes 3145744
  824.0 1.5 multiply_reduce_fusion
  825.4 142.0 %psum.7 = f32[]{:T(128)} all-reduce(f32[]{:T(128)} %multiply_reduce_fusion), channel_id=1, replica_groups=mesh['group'=8,'dp'=64] {'group','dp'}, use_global_device_ids=true, to_apply=%region_2.0 | all-reduce | flops 1 | bytes 8 | tf_op jit(solution)/shard_map/psum | solution.py:51
  968.2 1.5 fusion.50
  969.7 119.5 %all-gather.3.cloned.1.call-done = bf16[2,384,1024]{2,0,1:T(2,128)(2,1)} async-done(((bf16[2,6,1024]{2,0,1:T(2,128)(2,1)}), bf16[2,384,1024]{2,0,1:T(2,128)(2,1)}) %all-gather.3.cloned.1.call-update) | async-done | bytes 1572880 | tf_op jit(solution)/shard_map/all_gather | solution.py:61
  1089.2 3.2 fusion.35
  1092.4 1.0 fusion
  1094.4 0.6 convolution_convert_fusion.4
  1095.0 0.8 add_convert_fusion.3
  1095.9 0.6 convolution_convert_fusion.3
  1096.5 0.8 add_convert_fusion.2
  1097.9 0.8 add_convert_fusion.1
  1098.7 0.6 convolution_convert_fusion.1
  1099.3 0.8 add_convert_fusion
  1100.1 0.6 convolution_convert_fusion
  1100.7 0.8 multiply_convert_fusion
  1101.6 1.2 reshape.15
  1102.8 8.0 all-to-all-start
  1110.8 23.6 %all-to-all-done = bf16[64,6,1024]{2,1,0:T(8,128)(2,1)S(1)} async-done(((bf16[64,6,1024]{2,1,0:T(8,128)(2,1)}), bf16[64,6,1024]{2,1,0:T(8,128)(2,1)S(1)}, u32[]{:S(2)}, u32[]{:S(2)}) %all-to-all-start) | async-done | bytes 786464 | tf_op jit(solution)/shard_map/all_to_all | solution.py:67
  1134.4 1.5 convolution_convert_fusion.5
  1136.0 129.9 %all-gather.5.cloned.1.call-done = bf16[2,384,1024]{2,0,1:T(2,128)(2,1)} async-done(((bf16[2,6,1024]{2,0,1:T(2,128)(2,1)}), bf16[2,384,1024]{2,0,1:T(2,128)(2,1)}) %all-gather.5.cloned.1.call-update) | async-done | bytes 1572880 | tf_op jit(solution)/shard_map/all_gather | solution.py:73
  1265.9 3.0 copy.12
  (11 shorter events, 1.1 us)
Async XLA Ops:
  7.2 816.8 %all-reduce.3.cloned.1.call-start = ((), (), s32[]{:S(2)}) async-start(), calls=%async_computation.3 | async-start | bytes 6291456
  11.9 956.2 %copy-start = (f32[1,2,6,1024]{3,1,2,0:T(2,128)S(1)}, f32[1,2,6,1024]{3,1,2,0:T(2,128)}, u32[]{:S(2)}) copy-start(f32[1,2,6,1024]{3,1,2,0:T(2,128)} %param.3) | copy-start | bytes 147460
  11.9 1077.2 %all-gather.3.cloned.1.call-start = ((), (), s32[]{:S(2)}) async-start(), calls=%async_computation.1 | async-start | bytes 1597440 | tf_op jit(solution)/shard_map/all_gather | solution.py:61
  1102.8 31.7 %all-to-all-start = ((bf16[64,6,1024]{2,1,0:T(8,128)(2,1)}), bf16[64,6,1024]{2,1,0:T(8,128)(2,1)S(1)}, u32[]{:S(2)}, u32[]{:S(2)}) async-start(bf16[64,6,1024]{2,1,0:T(8,128)(2,1)} %reshape.15), calls=%async_computation | async-start | bytes 2097152 | tf_op jit(solution)/shard_map/all_to_all | solution.py:67
  1110.7 155.1 %all-gather.5.cloned.1.call-start = ((), (), s32[]{:S(2)}) async-start(), calls=%async_computation.2 | async-start | bytes 1597440 | tf_op jit(solution)/shard_map/all_gather | solution.py:73
Sparse Core Ops, SparseCore 0:
  12.1 811.8 all-reduce.2
  969.8 119.3 all-gather.2
  1136.1 129.7 all-gather.4
where the time goes:
time: 1280 us
  waiting for transfers between devices  1080 us (84%)
  blocking collectives  142 us (11%)
  between operations  15.9 us (1%)
    unnamed x4, waiting for transfers between devices  810 us
    psum x1, blocking collectives, shards(): square_sum = lax.psum(jnp.sum(summed * summed), ('group', 'dp'))  142 us
    all_gather x1, waiting for transfers between devices, shards(): update = lax.all_gather(row_blocks, 'dp', axis=1, tiled=True)  130 us
    all_gather x1, waiting for transfers between devices, shards(): gathered = lax.all_gather(blended, 'dp', axis=1, tiled=True)  120 us
  transfers between devices with their start and end apart: 4, of which 4 were waited for; matrix products, arithmetic and copies ran while one was open for 0% of the time, Pallas kernels for 0%

commit v1 on v0

v1 whole, which is shorter than its diff:
```python
import functools
import math

import jax
import jax.numpy as jnp
from jax import lax
from jax.experimental import pallas as pl
from jax.experimental.pallas import tpu as pltpu
from jax.sharding import PartitionSpec as P

MESH = pl.DeviceIdType.MESH

MATS = 2
ROWS = 384
COLS = 1024
ITERS = 5
GROUPS = 8

NX, NYH, NZ, NYL, NC = 4, 2, 8, 4, 2
SLAB = ROWS // (NX * NYH)
WIDE = COLS // NZ
TOP = SLAB * 2 // 3
REST = SLAB - TOP
OWN = SLAB // NZ
OWN_PAD = -(-OWN // 8) * 8

decay_rate = 0.95
coef_a = 3.4445
coef_b = -4.775
coef_c = 2.0315

bf16, f32 = jnp.bfloat16, jnp.float32


def place():
    d = lax.axis_index("dp")
    g = lax.axis_index("group")
    return d // (NYH * NZ), (d // NZ) % NYH, d % NZ, g // NC, g % NC


def dp_index(x, yh, z):
    return x * (NYH * NZ) + yh * NZ + z


def comm_kernel(p_ref, m_ref, xo_ref, own_a, own_b, got_a, got_b, sum_a, sum_b, got_a2, got_b2,
                m_out, m_got, q_out, q_got, lsem, ssem, rsem):
    x, yh, z, yl, core = place()
    counter = [0]

    def wrap(v, n):
        return lax.rem(v, n)

    def send(src, dst, device):
        i = counter[0]
        counter[0] += 1
        copy = pltpu.make_async_remote_copy(
            src_ref=src, dst_ref=dst, send_sem=ssem.at[i], recv_sem=rsem.at[i],
            device_id=device, device_id_type=MESH)
        copy.start()
        return copy

    x_peers = [(dx, 0) for dx in range(1, NX)]
    z_peers = list(range(1, NZ))
    yz_peers = [(dy, dz) for dy in range(NYH) for dz in range(NZ) if (dy, dz) != (0, 0)]
    xy_peers = [(dx, dy) for dx in range(NX) for dy in range(NYH) if (dx, dy) != (0, 0)]

    def at_z(dz):
        return {"dp": dp_index(x, yh, wrap(z + dz, NZ))}

    def at_yz(dy, dz):
        return {"dp": dp_index(x, wrap(yh + dy, NYH), wrap(z + dz, NZ))}

    def at_xy(dx, dy):
        return {"dp": dp_index(wrap(x + dx, NX), wrap(yh + dy, NYH), z)}

    def at_xc(dx, dc):
        return {"group": yl * NC + wrap(core + dc, NC), "dp": dp_index(wrap(x + dx, NX), yh, z)}

    def at_y(dy):
        y = wrap(yh * NYL + yl + dy, NYH * NYL)
        return {"group": lax.rem(y, NYL) * NC + core, "dp": dp_index(x, y // NYL, z)}

    xc_peers = [(dx, dc) for dx in range(NX) for dc in range(NC) if (dx, dc) != (0, 0)]
    y_peers = list(range(1, NYH * NYL))

    own_cols = pl.ds(pl.multiple_of(z * WIDE, WIDE), WIDE)

    def cols_of(zz):
        return pl.ds(pl.multiple_of(zz * WIDE, WIDE), WIDE)

    local_a = pltpu.make_async_copy(p_ref.at[:, x, :, 0:TOP, :], own_a, lsem.at[0])
    local_b = pltpu.make_async_copy(p_ref.at[:, :, :, TOP:SLAB, own_cols], own_b, lsem.at[1])
    local_a.start()
    local_b.start()

    targets = [at_yz(dy, dz) for dy, dz in yz_peers] + [at_xy(dx, dy) for dx, dy in xy_peers if dx != 0]
    targets += [at_xc(dx, dc) for dx, dc in xc_peers if dc != 0]
    targets += [at_y(dy) for dy in y_peers if dy % NYL != 0]
    barrier = pltpu.get_barrier_semaphore()
    for device in targets:
        pl.semaphore_signal(barrier, inc=1, device_id=device, device_id_type=MESH)
    m_out[...] = jnp.zeros_like(m_out)
    m_out[:, 0:OWN, :] = m_ref[...]
    pl.semaphore_wait(barrier, len(targets))

    sends = []
    a1 = [[], []]
    b1 = []
    b_order = list(z_peers)
    for m in range(MATS):
        for dx, _ in x_peers:
            a1[m].append(send(p_ref.at[m, wrap(x + dx, NX), :, 0:TOP, :], got_a.at[m, dx - 1], at_xy(dx, 0)))
            if b_order:
                dz = b_order.pop(0)
                b1.append(send(p_ref.at[:, :, :, TOP:SLAB, cols_of(wrap(z + dz, NZ))], got_b.at[dz - 1], at_z(dz)))
    while b_order:
        dz = b_order.pop(0)
        b1.append(send(p_ref.at[:, :, :, TOP:SLAB, cols_of(wrap(z + dz, NZ))], got_b.at[dz - 1], at_z(dz)))
    m1 = [send(m_out.at[:, :, cols_of(wrap(z + dz, NZ))], m_got.at[wrap(z, NZ)], at_z(dz)) for dz in z_peers]
    m_got[z] = m_out[:, :, own_cols]
    local_a.wait()
    local_b.wait()

    for m in range(MATS):
        for copy in a1[m]:
            copy.wait_recv()
        total = own_a[m].astype(f32)
        for j in range(NX - 1):
            total = total + got_a[m, j].astype(f32)
        sum_a[m] = total.astype(bf16)
    a2 = [send(sum_a.at[:, wrap(yh + dy, NYH), :, cols_of(wrap(z + dz, NZ))], got_a2.at[j], at_yz(dy, dz))
          for j, (dy, dz) in enumerate(yz_peers)]
    for copy in b1:
        copy.wait_recv()
    total = own_b[...].astype(f32)
    for j in range(NZ - 1):
        total = total + got_b[j].astype(f32)
    sum_b[...] = total.astype(bf16)
    b2 = [send(sum_b.at[:, wrap(x + dx, NX), wrap(yh + dy, NYH)], got_b2.at[j], at_xy(dx, dy))
          for j, (dx, dy) in enumerate(xy_peers)]

    for copy in m1:
        copy.wait_recv()
    row = lax.broadcasted_iota(jnp.int32, (SLAB, NZ * OWN_PAD), 0)
    slot = lax.broadcasted_iota(jnp.int32, (SLAB, NZ * OWN_PAD), 1)
    pick = ((slot // OWN_PAD) * OWN + slot % OWN_PAD == row) & (slot % OWN_PAD < OWN)
    pick = pick.astype(f32)
    m_block = [jnp.dot(pick, m_got[:, m].reshape(NZ * OWN_PAD, WIDE), preferred_element_type=f32,
                       precision=lax.Precision.HIGHEST) for m in range(MATS)]

    for copy in a2:
        copy.wait_recv()
    top = sum_a[:, yh, :, own_cols].astype(f32)
    for j in range(len(yz_peers)):
        top = top + got_a2[j].astype(f32)
    for copy in b2:
        copy.wait_recv()
    rest = sum_b[:, x, yh].astype(f32)
    for j in range(len(xy_peers)):
        rest = rest + got_b2[j].astype(f32)

    square = jnp.zeros((8, WIDE), f32)
    for m in range(MATS):
        for part in (top[m], rest[m]):
            for r in range(0, part.shape[0], 8):
                square = square + part[r:r + 8] * part[r:r + 8]
    slot = 0
    q_sends = []
    for stage, (peers, at) in enumerate(((z_peers, at_z), (xc_peers, lambda t: at_xc(*t)), (y_peers, at_y))):
        q_out[stage] = square
        stage_sends = [send(q_out.at[stage], q_got.at[slot + j], at(peer)) for j, peer in enumerate(peers)]
        for j, copy in enumerate(stage_sends):
            copy.wait_recv()
            square = square + q_got[slot + j]
        slot += len(peers)
        q_sends += stage_sends
    square_sum = jnp.sum(jnp.sum(square, axis=1, keepdims=True), axis=0, keepdims=True)
    entries = GROUPS * MATS * ROWS * COLS
    clip = jnp.minimum(1.0, math.sqrt(entries) / jnp.sqrt(square_sum + 1e-06))

    for m in range(MATS):
        for part, lo in ((top[m], 0), (rest[m], TOP)):
            n = part.shape[0]
            grad = clip * part
            momentum_new = decay_rate * m_block[m][lo:lo + n] + grad
            xo_ref[m, x, yh, lo:lo + n, own_cols] = (grad + decay_rate * momentum_new).astype(bf16)
    block_a = xo_ref.at[:, x, yh, 0:TOP, own_cols]
    block_b = xo_ref.at[:, x, yh, TOP:SLAB, own_cols]
    a3 = [send(block_a, block_a, at_yz(dy, dz)) for dy, dz in yz_peers]
    b3 = [send(block_b, block_b, at_xy(dx, dy)) for dx, dy in xy_peers]
    for copy in a3:
        copy.wait_recv()
    a4 = []
    for m in range(MATS):
        strip = xo_ref.at[m, x, :, 0:TOP, :]
        a4 += [send(strip, strip, at_xy(dx, 0)) for dx, _ in x_peers]
    for copy in b3:
        copy.wait_recv()
    strip = xo_ref.at[:, :, :, TOP:SLAB, own_cols]
    b4 = [send(strip, strip, at_z(dz)) for dz in z_peers]
    for copy in a4 + b4:
        copy.wait_recv()
    for copy in a1[0] + a1[1] + b1 + m1 + a2 + b2 + q_sends + a3 + b3 + a4 + b4:
        copy.wait_send()


def comm(partials, momentum):
    n_q = (NZ - 1) + (NX * NC - 1) + (NYH * NYL - 1)
    n_copies = 2 * (MATS * (NX - 1) + (NZ - 1) + (NYH * NZ - 1) + (NX * NYH - 1)) + (NZ - 1) + n_q
    return pl.pallas_call(
        comm_kernel,
        name="reduce_blend_gather",
        out_shape=jax.ShapeDtypeStruct((MATS, NX, NYH, SLAB, COLS), bf16),
        in_specs=[pl.BlockSpec(memory_space=pl.ANY), pl.BlockSpec(memory_space=pltpu.VMEM)],
        out_specs=pl.BlockSpec(memory_space=pltpu.VMEM),
        scratch_shapes=[
            pltpu.VMEM((MATS, NYH, TOP, COLS), bf16),
            pltpu.VMEM((MATS, NX, NYH, REST, WIDE), bf16),
            pltpu.VMEM((MATS, NX - 1, NYH, TOP, COLS), bf16),
            pltpu.VMEM((NZ - 1, MATS, NX, NYH, REST, WIDE), bf16),
            pltpu.VMEM((MATS, NYH, TOP, COLS), bf16),
            pltpu.VMEM((MATS, NX, NYH, REST, WIDE), bf16),
            pltpu.VMEM((NYH * NZ - 1, MATS, TOP, WIDE), bf16),
            pltpu.VMEM((NX * NYH - 1, MATS, REST, WIDE), bf16),
            pltpu.VMEM((MATS, OWN_PAD, COLS), f32),
            pltpu.VMEM((NZ, MATS, OWN_PAD, WIDE), f32),
            pltpu.VMEM((3, 8, WIDE), f32),
            pltpu.VMEM((n_q, 8, WIDE), f32),
            pltpu.SemaphoreType.DMA((2,)),
            pltpu.SemaphoreType.DMA((n_copies,)),
            pltpu.SemaphoreType.DMA((n_copies,)),
        ],
        compiler_params=pltpu.CompilerParams(
            collective_id=0, has_side_effects=True, vmem_limit_bytes=32 << 20),
        cost_estimate=pl.CostEstimate(flops=10_000_000, bytes_accessed=8_000_000, transcendentals=0),
    )(partials, momentum)


def newton_kernel(x_ref, m_ref, u_ref, mo_ref, cur):
    x, yh, z, _, _ = place()
    final_scale = 0.2 * math.sqrt(max(ROWS, COLS))

    row = lax.broadcasted_iota(jnp.int32, (OWN_PAD, SLAB), 0)
    col = lax.broadcasted_iota(jnp.int32, (OWN_PAD, SLAB), 1)
    pick = ((col == z * OWN + row) & (row < OWN)).astype(f32).astype(bf16)
    for m in range(MATS):
        mine = jnp.dot(pick, x_ref[m, x, yh], preferred_element_type=f32)[0:OWN]
        old = m_ref[m]
        grad = (mine - (decay_rate * decay_rate) * old) * (1.0 / (1.0 + decay_rate))
        mo_ref[m] = decay_rate * old + grad

    for m in range(MATS):
        full = x_ref[m].reshape(ROWS, COLS).astype(f32)
        norm = jnp.sqrt(jnp.sum(jnp.sum(full * full, axis=1, keepdims=True), axis=0, keepdims=True))
        cur[m] = (full * (1.0 / (norm + 1e-07))).astype(bf16)

    def poly(m):
        here = cur[m]
        gram = lax.dot_general(here, here, (((1,), (1,)), ((), ())), preferred_element_type=f32).astype(bf16)
        square = jnp.dot(gram, gram, preferred_element_type=f32)
        return (coef_b * gram.astype(f32) + coef_c * square).astype(bf16)

    def step(_, carry):
        polys = [poly(m) for m in range(MATS)]
        for m in range(MATS):
            here = cur[m]
            cur[m] = (coef_a * here.astype(f32) + jnp.dot(polys[m], here, preferred_element_type=f32)).astype(bf16)
        return carry

    lax.fori_loop(0, ITERS - 1, step, 0)
    polys = [poly(m) for m in range(MATS)]
    for m in range(MATS):
        here = cur[m]
        last = coef_a * here.astype(f32) + jnp.dot(polys[m], here, preferred_element_type=f32)
        u_ref[m] = (last * final_scale).astype(bf16)


def newton(blended, momentum):
    vmem = pl.BlockSpec(memory_space=pltpu.VMEM)
    return pl.pallas_call(
        newton_kernel,
        name="newton_schulz",
        out_shape=(jax.ShapeDtypeStruct((MATS, ROWS, COLS), bf16), jax.ShapeDtypeStruct((MATS, OWN, COLS), f32)),
        in_specs=[vmem, vmem],
        out_specs=(vmem, vmem),
        scratch_shapes=[pltpu.VMEM((MATS, ROWS, COLS), bf16)],
        compiler_params=pltpu.CompilerParams(vmem_limit_bytes=40 << 20),
        cost_estimate=pl.CostEstimate(flops=7_200_000_000, bytes_accessed=3_200_000, transcendentals=0),
    )(blended, momentum)


def shards(partials, momentum):
    parts = partials.reshape(MATS, NX, NYH, SLAB, COLS)
    old = momentum.reshape(MATS, OWN, COLS)
    blended = comm(parts, old)
    update, momentum_out = newton(blended, old)
    return update[None], momentum_out[None]


def solution(mesh):
    in_specs = (P("group", "dp", None, None, None), P("group", None, "dp", None))
    out_specs = (P("group", None, None, None), P("group", None, "dp", None))
    return jax.shard_map(shards, mesh=mesh, in_specs=in_specs, out_specs=out_specs, check_vma=False)
```

time: 1280 us -> 98.8 us (0.08)
  waiting for transfers between devices: 1080 us -> 0 us
  blocking collectives: 142 us -> 0 us
  Pallas kernels: 0 us -> 95.1 us
  between operations: 15.9 us -> 0.65 us
    unnamed x4 -> x0, waiting for transfers between devices: 810 us -> none
    all_gather x2 -> x0, waiting for transfers between devices: 249 us -> none  [the longest x1 130 us: shards(): update = lax.all_gather(row_blocks, 'dp', axis=1, tiled=True)]
    psum x1 -> x0, blocking collectives: 142 us -> none  [shards(): square_sum = lax.psum(jnp.sum(summed * summed), ('group', 'dp'))]
    pallas_call x0 -> x2, Pallas kernels: none -> 95.1 us  [the longest x1 81.2 us: comm(): pl.pallas_call(comm_kernel, name='reduce_blend_gather', out_shape=jax.Sha...]
    all_to_all x1 -> x0, waiting for transfers between devices: 23.6 us -> none  [shards(): lax.all_to_all(result.reshape(dp_count, block_rows, COLS), 'dp', split_ax...]
  transfers between devices with their start and end apart: 4 -> 0, of which waited for: 4 -> 0; matrix products, arithmetic and copies ran while one was open for 0% -> 0% of each run, Pallas kernels for 0% -> 0%
where the time goes in v1:
time: 98.8 us; the launch traced here: 98.6 us
  Pallas kernels  95.1 us (96%)
  local copies, waits for them, and re-layouts  2.88 us (3%)
    pallas_call x1, Pallas kernels, comm(): pl.pallas_call(comm_kernel, name='reduce_blend_gather', out_shape=jax.Sha...  81.2 us
    pallas_call x1, Pallas kernels, newton(): pl.pallas_call(newton_kernel, name='newton_schulz', out_shape=(jax.ShapeD...  13.9 us
    unnamed x4, local copies, waits for them, and re-layouts  2.88 us

profile of v1, /device:TPU:1, one launch (start us, length us, event | category | flops | bytes accessed | tf_op | source)
XLA Modules:
  0.0 98.6 jit_solution(16360459453459476235)
XLA Ops:
  0.6 0.8 copy.7
  1.4 0.0 copy-start
  1.5 1.4 %copy-done = bf16[1,1,2,384,1024]{4,3,2,1,0:T(8,128)(2,1)S(1)} copy-done((bf16[1,1,2,384,1024]{4,3,2,1,0:T(8,128)(2,1)S(1)}, bf16[1,1,2,384,1024]{4,3,2,1,0:T(8,128)(2,1)}, u32[]{:S(2)}) %copy-start) | copy-done | bytes 1572888
  2.9 81.2 %reduce_blend_gather.1.x_ref = bf16[2,4,2,48,1024]{4,3,2,1,0:T(8,128)(2,1)S(1)} custom-call(bf16[2,4,2,48,1024]{4,3,2,1,0:T(8,128)(2,1)S(1)} %bitcast.6, f32[2,6,1024]{2,1,0:T(8,128)S(1)} %bitcast.7), custom_call_target="tpu_custom_call" | custom-call | flops 10000000 | bytes 8000000 | tf_op jit(solution)/shard_map/reduce_blend_gather/pallas_call | solution.py:210
  84.1 13.9 %newton_schulz.1 = (bf16[2,384,1024]{2,1,0:T(8,128)(2,1)}, f32[2,6,1024]{2,1,0:T(8,128)S(1)}) custom-call(bf16[2,4,2,48,1024]{4,3,2,1,0:T(8,128)(2,1)S(1)} %reduce_blend_gather.1.x_ref, f32[2,6,1024]{2,1,0:T(8,128)S(1)} %bitcast.8), custom_call_target="tpu_custom_call" | custom-call | flops 7200000000 | bytes 3200000 | tf_op jit(solution)/shard_map/newton_schulz/pallas_call | solution.py:280
  98.0 0.7 copy.5
Async XLA Ops:
  1.4 1.4 %copy-start = (bf16[1,1,2,384,1024]{4,3,2,1,0:T(8,128)(2,1)S(1)}, bf16[1,1,2,384,1024]{4,3,2,1,0:T(8,128)(2,1)}, u32[]{:S(2)}) copy-start(bf16[1,1,2,384,1024]{4,3,2,1,0:T(8,128)(2,1)} %param.2) | copy-start | bytes 4718596

commit v2 on v1

v2 whole, which is shorter than its diff:
```python
import functools
import math

import jax
import jax.numpy as jnp
from jax import lax
from jax.experimental import pallas as pl
from jax.experimental.pallas import tpu as pltpu
from jax.sharding import PartitionSpec as P

MESH = pl.DeviceIdType.MESH

MATS = 2
ROWS = 384
COLS = 1024
ITERS = 5
GROUPS = 8

NX, NYH, NZ, NYL, NC = 4, 2, 8, 4, 2
SLAB = ROWS // (NX * NYH)
WIDE = COLS // NZ
TOP = SLAB * 2 // 3
REST = SLAB - TOP
OWN = SLAB // NZ
OWN_PAD = -(-OWN // 8) * 8

decay_rate = 0.95
coef_a = 3.4445
coef_b = -4.775
coef_c = 2.0315

bf16, f32 = jnp.bfloat16, jnp.float32


def place():
    d = lax.axis_index("dp")
    g = lax.axis_index("group")
    return d // (NYH * NZ), (d // NZ) % NYH, d % NZ, g // NC, g % NC


def dp_index(x, yh, z):
    return x * (NYH * NZ) + yh * NZ + z


def comm_kernel(p_ref, m_ref, xo_ref, own_a, own_b, got_a, got_b, sum_a, sum_b, got_a2, got_b2,
                all_a, all_b, m_out, m_got, m_pair, m_a, m_b, q_got, lsem, ssem, rsem):
    x, yh, z, yl, core = place()
    counter = [0]

    def wrap(v, n):
        return lax.rem(v, n)

    sent = []

    def send(src, dst, device):
        i = counter[0]
        counter[0] += 1
        copy = pltpu.make_async_remote_copy(
            src_ref=src, dst_ref=dst, send_sem=ssem.at[i], recv_sem=rsem.at[i],
            device_id=device, device_id_type=MESH)
        copy.start()
        sent.append(copy)
        return copy

    x_peers = list(range(1, NX))
    z_peers = sorted(range(1, NZ), key=lambda d: -min(d, NZ - d))
    y_peers = list(range(1, NYH * NYL))
    yz_peers = [(dy, dz) for dy in range(NYH) for dz in range(NZ) if (dy, dz) != (0, 0)][::-1]
    xy_peers = [(dx, dy) for dx in range(NX) for dy in range(NYH) if (dx, dy) != (0, 0)][::-1]
    xc_peers = [(dx, dc) for dx in range(NX) for dc in range(NC) if (dx, dc) != (0, 0)]

    def at_z(dz):
        return {"dp": dp_index(x, yh, wrap(z + dz, NZ))}

    def at_x(dx):
        return {"dp": dp_index(wrap(x + dx, NX), yh, z)}

    def at_yz(t):
        return {"dp": dp_index(x, wrap(yh + t[0], NYH), wrap(z + t[1], NZ))}

    def at_xy(t):
        return {"dp": dp_index(wrap(x + t[0], NX), wrap(yh + t[1], NYH), z)}

    def at_xc(t):
        return {"group": yl * NC + wrap(core + t[1], NC), "dp": dp_index(wrap(x + t[0], NX), yh, z)}

    def at_y(dy):
        y = wrap(yh * NYL + yl + dy, NYH * NYL)
        return {"group": lax.rem(y, NYL) * NC + core, "dp": dp_index(x, y // NYL, z)}

    def cols_of(zz):
        return pl.ds(pl.multiple_of(zz * WIDE, WIDE), WIDE)

    own_cols = cols_of(z)

    local_a = pltpu.make_async_copy(p_ref.at[:, x, :, 0:TOP, :], own_a, lsem.at[0])
    local_b = pltpu.make_async_copy(p_ref.at[:, :, :, TOP:SLAB, own_cols], own_b, lsem.at[1])
    local_a.start()
    local_b.start()

    targets = [at_z(dz) for dz in z_peers] + [at_y(dy) for dy in y_peers] + [at_x(dx) for dx in x_peers]
    targets.append(at_xc((0, 1)))
    barrier = pltpu.get_barrier_semaphore()
    for device in targets:
        pl.semaphore_signal(barrier, inc=1, device_id=device, device_id_type=MESH)
    m_out[...] = jnp.zeros_like(m_out)
    for m in range(MATS):
        m_out[m, 0:OWN, :] = m_ref[:, m, :]
    m_got[z] = m_out[:, :, own_cols]
    pl.semaphore_wait(barrier, len(targets))

    m1 = [send(m_out.at[:, :, cols_of(wrap(z + dz, NZ))], m_got.at[z], at_z(dz)) for dz in z_peers]
    a1 = [[], []]
    b1 = []
    b_order = list(z_peers)

    def send_b():
        dz = b_order.pop(0)
        b1.append(send(p_ref.at[:, :, :, TOP:SLAB, cols_of(wrap(z + dz, NZ))], got_b.at[dz - 1], at_z(dz)))

    for m in range(MATS):
        for dx in x_peers:
            a1[m].append(send(p_ref.at[m, wrap(x + dx, NX), :, 0:TOP, :], got_a.at[m, dx - 1], at_x(dx)))
            if b_order:
                send_b()
    while b_order:
        send_b()

    row = lax.broadcasted_iota(jnp.int32, (SLAB, NZ * OWN_PAD), 0)
    slot = lax.broadcasted_iota(jnp.int32, (SLAB, NZ * OWN_PAD), 1)
    pick = ((slot // OWN_PAD) * OWN + slot % OWN_PAD == row) & (slot % OWN_PAD < OWN)
    pick = pick.astype(f32).astype(bf16)
    for copy in m1:
        copy.wait_recv()
    for m in range(MATS):
        block = jnp.dot(pick, m_got[:, m].reshape(NZ * OWN_PAD, WIDE).astype(bf16),
                        preferred_element_type=f32).astype(bf16)
        m_pair[m, yh] = block[0:TOP]
        m_b[m, x, yh] = block[TOP:SLAB]
    m2 = send(m_pair.at[:, yh], m_pair.at[:, yh], at_yz((1, 0)))

    local_a.wait()
    local_b.wait()
    for m in range(MATS):
        for copy in a1[m]:
            copy.wait_recv()
        total = own_a[m].astype(f32)
        for j in range(NX - 1):
            total = total + got_a[m, j].astype(f32)
        sum_a[m] = total.astype(bf16)
    a2 = [send(sum_a.at[:, wrap(yh + t[0], NYH), :, cols_of(wrap(z + t[1], NZ))], got_a2.at[j], at_yz(t))
          for j, t in enumerate(yz_peers)]
    for copy in b1:
        copy.wait_recv()
    total = own_b[...].astype(f32)
    for j in range(NZ - 1):
        total = total + got_b[j].astype(f32)
    sum_b[...] = total.astype(bf16)
    b2 = [send(sum_b.at[:, wrap(x + t[0], NX), wrap(yh + t[1], NYH)], got_b2.at[j], at_xy(t))
          for j, t in enumerate(xy_peers)]

    m4 = [send(m_b.at[:, x, yh], m_b.at[:, x, yh], at_xy(t)) for t in xy_peers]
    m2.wait_recv()
    m_a[:, :, :, own_cols] = m_pair[...]
    m3 = [send(m_pair, m_a.at[:, :, :, own_cols], at_z(dz)) for dz in z_peers]

    for copy in a2:
        copy.wait_recv()
    top = sum_a[:, yh, :, own_cols].astype(f32)
    for j in range(len(yz_peers)):
        top = top + got_a2[j].astype(f32)
    for copy in b2:
        copy.wait_recv()
    rest = sum_b[:, x, yh].astype(f32)
    for j in range(len(xy_peers)):
        rest = rest + got_b2[j].astype(f32)

    square = jnp.zeros((8, WIDE), f32)
    for m in range(MATS):
        for part in (top[m], rest[m]):
            for r in range(0, part.shape[0], 8):
                square = square + part[r:r + 8] * part[r:r + 8]

    def spread(stage, mine, peers, at):
        q_got[stage, mine] = square
        here = q_got.at[stage, mine]
        return [send(here, here, at(t)) for t in peers]

    def gather(stage, copies):
        for copy in copies:
            copy.wait_recv()
        total = q_got[stage, 0]
        for j in range(1, len(copies) + 1):
            total = total + q_got[stage, j]
        return total

    q = spread(0, z, z_peers, at_z)
    all_a[:, yh, :, own_cols] = top.astype(bf16)
    all_b[:, x, yh] = rest.astype(bf16)
    here = all_a.at[:, yh, :, own_cols]
    a3 = [send(here, here, at_yz(t)) for t in yz_peers]
    here = all_b.at[:, x, yh]
    b3 = [send(here, here, at_xy(t)) for t in xy_peers]
    square = gather(0, q)
    q = spread(1, x * NC + core, xc_peers, at_xc)
    square = gather(1, q)
    q = spread(2, yh * NYL + yl, y_peers, at_y)
    square = gather(2, q)
    square_sum = jnp.sum(jnp.sum(square, axis=1, keepdims=True), axis=0, keepdims=True)
    entries = GROUPS * MATS * ROWS * COLS
    clip = jnp.minimum(1.0, math.sqrt(entries) / jnp.sqrt(square_sum + 1e-06))
    scale = (1.0 + decay_rate) * clip

    for copy in m3 + a3:
        copy.wait_recv()
    a4 = []
    b4 = []
    for m in range(MATS):
        for j in range(NYH):
            xo_ref[m, x, j, 0:TOP, :] = (
                scale * all_a[m, j].astype(f32) + (decay_rate * decay_rate) * m_a[m, j].astype(f32)).astype(bf16)
        strip = xo_ref.at[m, x, :, 0:TOP, :]
        a4.append([send(strip, strip, at_x(dx)) for dx in x_peers])
        if m == 0:
            for copy in m4 + b3:
                copy.wait_recv()
        for i in range(NX):
            for j in range(NYH):
                xo_ref[m, i, j, TOP:SLAB, own_cols] = (
                    scale * all_b[m, i, j].astype(f32)
                    + (decay_rate * decay_rate) * m_b[m, i, j].astype(f32)).astype(bf16)
        strip = xo_ref.at[m, :, :, TOP:SLAB, own_cols]
        b4.append([send(strip, strip, at_z(dz)) for dz in z_peers])
    for m in range(MATS):
        for copy in a4[m] + b4[m]:
            copy.wait_recv()
    for copy in sent:
        copy.wait_send()


def comm(partials, momentum):
    z_n, yz_n, xy_n = NZ - 1, NYH * NZ - 1, NX * NYH - 1
    n_copies = 4 * (NX - 1) + 3 * z_n + 2 * yz_n + 2 * xy_n + 2 * z_n + xy_n + 1 + z_n + (NX * NC - 1) + (NYH * NYL - 1)
    return pl.pallas_call(
        comm_kernel,
        name="reduce_blend_gather",
        out_shape=jax.ShapeDtypeStruct((MATS, NX, NYH, SLAB, COLS), bf16),
        in_specs=[pl.BlockSpec(memory_space=pltpu.HBM), pl.BlockSpec(memory_space=pltpu.VMEM)],
        out_specs=pl.BlockSpec(memory_space=pltpu.VMEM),
        scratch_shapes=[
            pltpu.VMEM((MATS, NYH, TOP, COLS), bf16),
            pltpu.VMEM((MATS, NX, NYH, REST, WIDE), bf16),
            pltpu.VMEM((MATS, NX - 1, NYH, TOP, COLS), bf16),
            pltpu.VMEM((NZ - 1, MATS, NX, NYH, REST, WIDE), bf16),
            pltpu.VMEM((MATS, NYH, TOP, COLS), bf16),
            pltpu.VMEM((MATS, NX, NYH, REST, WIDE), bf16),
            pltpu.VMEM((NYH * NZ - 1, MATS, TOP, WIDE), bf16),
            pltpu.VMEM((NX * NYH - 1, MATS, REST, WIDE), bf16),
            pltpu.VMEM((MATS, NYH, TOP, COLS), bf16),
            pltpu.VMEM((MATS, NX, NYH, REST, WIDE), bf16),
            pltpu.VMEM((MATS, OWN_PAD, COLS), f32),
            pltpu.VMEM((NZ, MATS, OWN_PAD, WIDE), f32),
            pltpu.VMEM((MATS, NYH, TOP, WIDE), bf16),
            pltpu.VMEM((MATS, NYH, TOP, COLS), bf16),
            pltpu.VMEM((MATS, NX, NYH, REST, WIDE), bf16),
            pltpu.VMEM((3, 8, 8, WIDE), f32),
            pltpu.SemaphoreType.DMA((2,)),
            pltpu.SemaphoreType.DMA((n_copies,)),
            pltpu.SemaphoreType.DMA((n_copies,)),
        ],
        compiler_params=pltpu.CompilerParams(
            collective_id=0, has_side_effects=True, vmem_limit_bytes=32 << 20),
        cost_estimate=pl.CostEstimate(flops=10_000_000, bytes_accessed=8_000_000, transcendentals=0),
    )(partials, momentum)


def newton_kernel(x_ref, m_ref, u_ref, mo_ref, cur):
    x, yh, z, _, _ = place()
    final_scale = 0.2 * math.sqrt(max(ROWS, COLS))

    row = lax.broadcasted_iota(jnp.int32, (OWN_PAD, SLAB), 0)
    col = lax.broadcasted_iota(jnp.int32, (OWN_PAD, SLAB), 1)
    pick = ((col == z * OWN + row) & (row < OWN)).astype(f32).astype(bf16)
    for m in range(MATS):
        mine = jnp.dot(pick, x_ref[m, x, yh], preferred_element_type=f32)[0:OWN]
        old = m_ref[:, m, :]
        grad = (mine - (decay_rate * decay_rate) * old) * (1.0 / (1.0 + decay_rate))
        mo_ref[:, m, :] = decay_rate * old + grad

    for m in range(MATS):
        full = x_ref[m].reshape(ROWS, COLS).astype(f32)
        norm = jnp.sqrt(jnp.sum(jnp.sum(full * full, axis=1, keepdims=True), axis=0, keepdims=True))
        cur[m] = (full * (1.0 / (norm + 1e-07))).astype(bf16)

    def poly(m):
        here = cur[m]
        gram = lax.dot_general(here, here, (((1,), (1,)), ((), ())), preferred_element_type=f32).astype(bf16)
        square = jnp.dot(gram, gram, preferred_element_type=f32)
        return (coef_b * gram.astype(f32) + coef_c * square).astype(bf16)

    def step(_, carry):
        polys = [poly(m) for m in range(MATS)]
        for m in range(MATS):
            here = cur[m]
            cur[m] = (coef_a * here.astype(f32) + jnp.dot(polys[m], here, preferred_element_type=f32)).astype(bf16)
        return carry

    lax.fori_loop(0, ITERS - 1, step, 0)
    polys = [poly(m) for m in range(MATS)]
    for m in range(MATS):
        here = cur[m]
        last = coef_a * here.astype(f32) + jnp.dot(polys[m], here, preferred_element_type=f32)
        u_ref[m] = (last * final_scale).astype(bf16)


def newton(blended, momentum):
    vmem = pl.BlockSpec(memory_space=pltpu.VMEM)
    return pl.pallas_call(
        newton_kernel,
        name="newton_schulz",
        out_shape=(jax.ShapeDtypeStruct((MATS, ROWS, COLS), bf16), jax.ShapeDtypeStruct((OWN, MATS, COLS), f32)),
        in_specs=[vmem, vmem],
        out_specs=(vmem, vmem),
        scratch_shapes=[pltpu.VMEM((MATS, ROWS, COLS), bf16)],
        compiler_params=pltpu.CompilerParams(vmem_limit_bytes=40 << 20),
        cost_estimate=pl.CostEstimate(flops=7_200_000_000, bytes_accessed=3_200_000, transcendentals=0),
    )(blended, momentum)


def shards(partials, momentum):
    parts = partials.reshape(MATS, NX, NYH, SLAB, COLS)
    old = jnp.transpose(momentum[0], (1, 0, 2))
    blended = comm(parts, old)
    update, momentum_out = newton(blended, old)
    return update[None], jnp.transpose(momentum_out, (1, 0, 2))[None]


def solution(mesh):
    in_specs = (P("group", "dp", None, None, None), P("group", None, "dp", None))
    out_specs = (P("group", None, None, None), P("group", None, "dp", None))
    return jax.shard_map(shards, mesh=mesh, in_specs=in_specs, out_specs=out_specs, check_vma=False)
```

time: 98.8 us -> 86.6 us (0.88)
  Pallas kernels: 95.1 us -> 83.5 us
    pallas_call x1, Pallas kernels: 81.2 us -> 69.6 us  [comm(): pl.pallas_call(comm_kernel, name='reduce_blend_gather', out_shape=jax.Sha...]
    unnamed x4 -> x6, local copies, waits for them, and re-layouts: 2.88 us -> 2.2 us
where the time goes in v2:
time: 86.6 us; the launch traced here: 86.4 us
  Pallas kernels  83.5 us (96%)
  local copies, waits for them, and re-layouts  2.2 us (3%)
    pallas_call x1, Pallas kernels, comm(): pl.pallas_call(comm_kernel, name='reduce_blend_gather', out_shape=jax.Sha...  69.6 us
    pallas_call x1, Pallas kernels, newton(): pl.pallas_call(newton_kernel, name='newton_schulz', out_shape=(jax.ShapeD...  13.9 us
    unnamed x6, local copies, waits for them, and re-layouts  2.2 us

profile of v2, /device:TPU:1, one launch (start us, length us, event | category | flops | bytes accessed | tf_op | source)
XLA Modules:
  0.0 86.4 jit_solution(9954130607247685356)
XLA Ops:
  0.6 0.0 copy-start
  0.6 1.4 %copy-done = bf16[1,1,2,384,1024]{4,3,2,1,0:T(8,128)(2,1)S(1)} copy-done((bf16[1,1,2,384,1024]{4,3,2,1,0:T(8,128)(2,1)S(1)}, bf16[1,1,2,384,1024]{4,3,2,1,0:T(8,128)(2,1)}, u32[]{:S(2)}) %copy-start) | copy-done | bytes 1572888
  2.0 0.0 copy-start.1
  2.0 0.8 copy-done.1
  2.8 0.0 copy-start.2
  2.8 69.6 %reduce_blend_gather.1.x_ref = bf16[2,4,2,48,1024]{4,3,2,1,0:T(8,128)(2,1)S(1)} custom-call(bf16[2,4,2,48,1024]{4,3,2,1,0:T(8,128)(2,1)S(1)} %bitcast.8, f32[6,2,1024]{2,1,0:T(2,128)S(1)} %bitcast.9), custom_call_target="tpu_custom_call" | custom-call | flops 10000000 | bytes 8000000 | tf_op jit(solution)/shard_map/reduce_blend_gather/pallas_call | solution.py:244
  72.4 0.0 copy-done.2
  72.5 13.9 %newton_schulz.1 = (bf16[2,384,1024]{2,1,0:T(8,128)(2,1)}, f32[6,2,1024]{2,1,0:T(2,128)}) custom-call(bf16[2,4,2,48,1024]{4,3,2,1,0:T(8,128)(2,1)S(1)} %reduce_blend_gather.1.x_ref, f32[6,2,1024]{2,1,0:T(2,128)S(1)} %bitcast.10), custom_call_target="tpu_custom_call" | custom-call | flops 7200000000 | bytes 3200000 | tf_op jit(solution)/shard_map/newton_schulz/pallas_call | solution.py:318
Async XLA Ops:
  0.6 1.4 %copy-start = (bf16[1,1,2,384,1024]{4,3,2,1,0:T(8,128)(2,1)S(1)}, bf16[1,1,2,384,1024]{4,3,2,1,0:T(8,128)(2,1)}, u32[]{:S(2)}) copy-start(bf16[1,1,2,384,1024]{4,3,2,1,0:T(8,128)(2,1)} %param.2) | copy-start | bytes 4718596
  2.0 0.8 copy-start.1
  2.8 69.6 %copy-start.2 = (f32[1,2,6,1024]{3,1,2,0:T(2,128)S(1)}, f32[1,2,6,1024]{3,1,2,0:T(2,128)}, u32[]{:S(2)}) copy-start(f32[1,2,6,1024]{3,1,2,0:T(2,128)} %param.3) | copy-start | bytes 147460

commit v3 on v2

--- a/solution.py
+++ b/solution.py
@@ -14,6 +14,7 @@
 ROWS = 384
 COLS = 1024
 ITERS = 5
+EARLY = 4
 GROUPS = 8
 
 NX, NYH, NZ, NYL, NC = 4, 2, 8, 4, 2
@@ -42,9 +43,26 @@
     return x * (NYH * NZ) + yh * NZ + z
 
 
-def comm_kernel(p_ref, m_ref, xo_ref, own_a, own_b, got_a, got_b, sum_a, sum_b, got_a2, got_b2,
+def normalized(block):
+    full = block.astype(f32)
+    norm = jnp.sqrt(jnp.sum(jnp.sum(full * full, axis=1, keepdims=True), axis=0, keepdims=True))
+    return (full * (1.0 / (norm + 1e-07))).astype(bf16)
+
+
+def poly_of(here):
+    gram = lax.dot_general(here, here, (((1,), (1,)), ((), ())), preferred_element_type=f32).astype(bf16)
+    square = jnp.dot(gram, gram, preferred_element_type=f32)
+    return (coef_b * gram.astype(f32) + coef_c * square).astype(bf16)
+
+
+def stepped(here):
+    return coef_a * here.astype(f32) + jnp.dot(poly_of(here), here, preferred_element_type=f32)
+
+
+def comm_kernel(p_ref, m_ref, x1_ref, y0_ref, mo_ref, x0_ref, own_a, own_b, got_a, got_b, sum_a, sum_b, got_a2, got_b2,
                 all_a, all_b, m_out, m_got, m_pair, m_a, m_b, q_got, lsem, ssem, rsem):
     x, yh, z, yl, core = place()
+    xs = (x0_ref, x1_ref)
     counter = [0]
 
     def wrap(v, n):
@@ -141,6 +159,7 @@
 
     local_a.wait()
     local_b.wait()
+    a2 = []
     for m in range(MATS):
         for copy in a1[m]:
             copy.wait_recv()
@@ -148,8 +167,8 @@
         for j in range(NX - 1):
             total = total + got_a[m, j].astype(f32)
         sum_a[m] = total.astype(bf16)
-    a2 = [send(sum_a.at[:, wrap(yh + t[0], NYH), :, cols_of(wrap(z + t[1], NZ))], got_a2.at[j], at_yz(t))
-          for j, t in enumerate(yz_peers)]
+        a2 += [send(sum_a.at[m, wrap(yh + t[0], NYH), :, cols_of(wrap(z + t[1], NZ))], got_a2.at[j, m], at_yz(t))
+               for j, t in enumerate(yz_peers)]
     for copy in b1:
         copy.wait_recv()
     total = own_b[...].astype(f32)
@@ -217,37 +236,54 @@
     b4 = []
     for m in range(MATS):
         for j in range(NYH):
-            xo_ref[m, x, j, 0:TOP, :] = (
+            xs[m][x, j, 0:TOP, :] = (
                 scale * all_a[m, j].astype(f32) + (decay_rate * decay_rate) * m_a[m, j].astype(f32)).astype(bf16)
-        strip = xo_ref.at[m, x, :, 0:TOP, :]
+        strip = xs[m].at[x, :, 0:TOP, :]
         a4.append([send(strip, strip, at_x(dx)) for dx in x_peers])
         if m == 0:
             for copy in m4 + b3:
                 copy.wait_recv()
         for i in range(NX):
             for j in range(NYH):
-                xo_ref[m, i, j, TOP:SLAB, own_cols] = (
+                xs[m][i, j, TOP:SLAB, own_cols] = (
                     scale * all_b[m, i, j].astype(f32)
                     + (decay_rate * decay_rate) * m_b[m, i, j].astype(f32)).astype(bf16)
-        strip = xo_ref.at[m, :, :, TOP:SLAB, own_cols]
+        strip = xs[m].at[:, :, TOP:SLAB, own_cols]
         b4.append([send(strip, strip, at_z(dz)) for dz in z_peers])
-    for m in range(MATS):
-        for copy in a4[m] + b4[m]:
-            copy.wait_recv()
+
+    for copy in a4[0] + b4[0]:
+        copy.wait_recv()
+    y0_ref[...] = normalized(x0_ref[...].reshape(ROWS, COLS))
+    for _ in range(EARLY):
+        y0_ref[...] = stepped(y0_ref[...]).astype(bf16)
+
+    for copy in a4[1] + b4[1]:
+        copy.wait_recv()
+
+    row = lax.broadcasted_iota(jnp.int32, (OWN_PAD, SLAB), 0)
+    col = lax.broadcasted_iota(jnp.int32, (OWN_PAD, SLAB), 1)
+    pick = ((col == z * OWN + row) & (row < OWN)).astype(f32).astype(bf16)
+    for m in range(MATS):
+        mine = jnp.dot(pick, xs[m][x, yh], preferred_element_type=f32)[0:OWN]
+        old = m_ref[:, m, :]
+        grad = (mine - (decay_rate * decay_rate) * old) * (1.0 / (1.0 + decay_rate))
+        mo_ref[:, m, :] = decay_rate * old + grad
     for copy in sent:
         copy.wait_send()
 
 
 def comm(partials, momentum):
     z_n, yz_n, xy_n = NZ - 1, NYH * NZ - 1, NX * NYH - 1
-    n_copies = 4 * (NX - 1) + 3 * z_n + 2 * yz_n + 2 * xy_n + 2 * z_n + xy_n + 1 + z_n + (NX * NC - 1) + (NYH * NYL - 1)
+    n_copies = 4 * (NX - 1) + 3 * z_n + 3 * yz_n + 2 * xy_n + 2 * z_n + xy_n + 1 + z_n + (NX * NC - 1) + (NYH * NYL - 1)
     return pl.pallas_call(
         comm_kernel,
         name="reduce_blend_gather",
-        out_shape=jax.ShapeDtypeStruct((MATS, NX, NYH, SLAB, COLS), bf16),
+        out_shape=(jax.ShapeDtypeStruct((NX, NYH, SLAB, COLS), bf16), jax.ShapeDtypeStruct((ROWS, COLS), bf16),
+                   jax.ShapeDtypeStruct((OWN, MATS, COLS), f32)),
         in_specs=[pl.BlockSpec(memory_space=pltpu.HBM), pl.BlockSpec(memory_space=pltpu.VMEM)],
-        out_specs=pl.BlockSpec(memory_space=pltpu.VMEM),
+        out_specs=(pl.BlockSpec(memory_space=pltpu.VMEM),) * 3,
         scratch_shapes=[
+            pltpu.VMEM((NX, NYH, SLAB, COLS), bf16),
             pltpu.VMEM((MATS, NYH, TOP, COLS), bf16),
             pltpu.VMEM((MATS, NX, NYH, REST, WIDE), bf16),
             pltpu.VMEM((MATS, NX - 1, NYH, TOP, COLS), bf16),
@@ -270,68 +306,57 @@
         ],
         compiler_params=pltpu.CompilerParams(
             collective_id=0, has_side_effects=True, vmem_limit_bytes=32 << 20),
-        cost_estimate=pl.CostEstimate(flops=10_000_000, bytes_accessed=8_000_000, transcendentals=0),
+        cost_estimate=pl.CostEstimate(flops=2_900_000_000, bytes_accessed=8_000_000, transcendentals=0),
     )(partials, momentum)
 
 
-def newton_kernel(x_ref, m_ref, u_ref, mo_ref, cur):
-    x, yh, z, _, _ = place()
+def newton_kernel(x1_ref, y0_ref, mi_ref, u_ref, mo_ref, cur, done, sem):
     final_scale = 0.2 * math.sqrt(max(ROWS, COLS))
-
-    row = lax.broadcasted_iota(jnp.int32, (OWN_PAD, SLAB), 0)
-    col = lax.broadcasted_iota(jnp.int32, (OWN_PAD, SLAB), 1)
-    pick = ((col == z * OWN + row) & (row < OWN)).astype(f32).astype(bf16)
-    for m in range(MATS):
-        mine = jnp.dot(pick, x_ref[m, x, yh], preferred_element_type=f32)[0:OWN]
-        old = m_ref[:, m, :]
-        grad = (mine - (decay_rate * decay_rate) * old) * (1.0 / (1.0 + decay_rate))
-        mo_ref[:, m, :] = decay_rate * old + grad
-
-    for m in range(MATS):
-        full = x_ref[m].reshape(ROWS, COLS).astype(f32)
-        norm = jnp.sqrt(jnp.sum(jnp.sum(full * full, axis=1, keepdims=True), axis=0, keepdims=True))
-        cur[m] = (full * (1.0 / (norm + 1e-07))).astype(bf16)
-
-    def poly(m):
-        here = cur[m]
-        gram = lax.dot_general(here, here, (((1,), (1,)), ((), ())), preferred_element_type=f32).astype(bf16)
-        square = jnp.dot(gram, gram, preferred_element_type=f32)
-        return (coef_b * gram.astype(f32) + coef_c * square).astype(bf16)
-
-    def step(_, carry):
-        polys = [poly(m) for m in range(MATS)]
-        for m in range(MATS):
+    mo_ref[...] = mi_ref[...]
+    copies = []
+
+    def finish(m, value):
+        done[m] = (value * final_scale).astype(bf16)
+        copies.append(pltpu.make_async_copy(done.at[m], u_ref.at[m], sem.at[m]))
+        copies[-1].start()
+
+    cur[0] = y0_ref[...]
+    cur[1] = normalized(x1_ref[...].reshape(ROWS, COLS))
+    left = [ITERS - EARLY, ITERS]
+    for _ in range(ITERS):
+        work = [m for m in range(MATS) if left[m] > 0]
+        polys = {m: poly_of(cur[m]) for m in work}
+        for m in work:
             here = cur[m]
-            cur[m] = (coef_a * here.astype(f32) + jnp.dot(polys[m], here, preferred_element_type=f32)).astype(bf16)
-        return carry
-
-    lax.fori_loop(0, ITERS - 1, step, 0)
-    polys = [poly(m) for m in range(MATS)]
-    for m in range(MATS):
-        here = cur[m]
-        last = coef_a * here.astype(f32) + jnp.dot(polys[m], here, preferred_element_type=f32)
-        u_ref[m] = (last * final_scale).astype(bf16)
-
-
-def newton(blended, momentum):
+            value = coef_a * here.astype(f32) + jnp.dot(polys[m], here, preferred_element_type=f32)
+            left[m] -= 1
+            if left[m] > 0:
+                cur[m] = value.astype(bf16)
+            else:
+                finish(m, value)
+    for copy in copies:
+        copy.wait()
+
+
+def newton(x1, y0, momentum_out):
     vmem = pl.BlockSpec(memory_space=pltpu.VMEM)
     return pl.pallas_call(
         newton_kernel,
         name="newton_schulz",
         out_shape=(jax.ShapeDtypeStruct((MATS, ROWS, COLS), bf16), jax.ShapeDtypeStruct((OWN, MATS, COLS), f32)),
-        in_specs=[vmem, vmem],
-        out_specs=(vmem, vmem),
-        scratch_shapes=[pltpu.VMEM((MATS, ROWS, COLS), bf16)],
+        in_specs=[vmem, vmem, vmem],
+        out_specs=(pl.BlockSpec(memory_space=pltpu.HBM), vmem),
+        scratch_shapes=[pltpu.VMEM((MATS, ROWS, COLS), bf16), pltpu.VMEM((MATS, ROWS, COLS), bf16),
+                        pltpu.SemaphoreType.DMA((MATS,))],
         compiler_params=pltpu.CompilerParams(vmem_limit_bytes=40 << 20),
-        cost_estimate=pl.CostEstimate(flops=7_200_000_000, bytes_accessed=3_200_000, transcendentals=0),
-    )(blended, momentum)
+        cost_estimate=pl.CostEstimate(flops=4_300_000_000, bytes_accessed=3_200_000, transcendentals=0),
+    )(x1, y0, momentum_out)
 
 
 def shards(partials, momentum):
     parts = partials.reshape(MATS, NX, NYH, SLAB, COLS)
     old = jnp.transpose(momentum[0], (1, 0, 2))
-    blended = comm(parts, old)
-    update, momentum_out = newton(blended, old)
+    update, momentum_out = newton(*comm(parts, old))
     return update[None], jnp.transpose(momentum_out, (1, 0, 2))[None]
 
 

time: 86.6 us -> 81.5 us (0.941)
  Pallas kernels: 83.5 us -> 77.9 us
    pallas_call x1, Pallas kernels: 13.9 us -> 8.63 us  [newton(): pl.pallas_call(newton_kernel, name='newton_schulz', out_shape=(jax.ShapeD...]
    unnamed x6 -> x4, local copies, waits for them, and re-layouts: 2.2 us -> 2.2 us
where the time goes in v3:
time: 81.5 us; the launch traced here: 80.8 us
  Pallas kernels  77.9 us (96%)
  local copies, waits for them, and re-layouts  2.2 us (3%)
    pallas_call x1, Pallas kernels, comm(): pl.pallas_call(comm_kernel, name='reduce_blend_gather', out_shape=(jax.Sh...  69.3 us
    pallas_call x1, Pallas kernels, newton(): pl.pallas_call(newton_kernel, name='newton_schulz', out_shape=(jax.ShapeD...  8.63 us
    unnamed x4, local copies, waits for them, and re-layouts  2.2 us

profile of v3, /device:TPU:1, one launch (start us, length us, event | category | flops | bytes accessed | tf_op | source)
XLA Modules:
  0.0 80.8 jit_solution(10682830895038041256)
XLA Ops:
  0.6 0.0 copy-start
  0.6 1.4 %copy-done = bf16[1,1,2,384,1024]{4,3,2,1,0:T(8,128)(2,1)S(1)} copy-done((bf16[1,1,2,384,1024]{4,3,2,1,0:T(8,128)(2,1)S(1)}, bf16[1,1,2,384,1024]{4,3,2,1,0:T(8,128)(2,1)}, u32[]{:S(2)}) %copy-start) | copy-done | bytes 1572888
  2.0 0.0 copy-start.1
  2.0 0.8 copy-done.1
  2.8 69.3 %reduce_blend_gather.1 = (bf16[4,2,48,1024]{3,2,1,0:T(8,128)(2,1)S(1)}, bf16[384,1024]{1,0:T(8,128)(2,1)S(1)}, f32[6,2,1024]{2,1,0:T(2,128)S(1)}) custom-call(bf16[2,4,2,48,1024]{4,3,2,1,0:T(8,128)(2,1)S(1)} %bitcast.8, f32[6,2,1024]{2,1,0:T(2,128)S(1)} %bitcast.9), custom_call_target="tpu_custom_call" | custom-call | flops 2900000000 | bytes 8000000 | tf_op jit(solution)/shard_map/reduce_blend_gather/pallas_call | solution.py:278
  72.1 8.6 %newton_schulz.1 = (bf16[2,384,1024]{2,1,0:T(8,128)(2,1)}, f32[6,2,1024]{2,1,0:T(2,128)}) custom-call(bf16[4,2,48,1024]{3,2,1,0:T(8,128)(2,1)S(1)} %get-tuple-element.7.x1_ref, bf16[384,1024]{1,0:T(8,128)(2,1)S(1)} %get-tuple-element.8.y0_ref, f32[6,2,1024]{2,1,0:T(2,128)S(1)} %get-tuple-element.9.mi_ref), custom_call_target="tpu_custom_call" | custom-call | flops 4300000256 | bytes 3200000 | tf_op jit(solution)/shard_map/newton_schulz/pallas_call | solution.py:343
Async XLA Ops:
  0.6 1.4 %copy-start = (bf16[1,1,2,384,1024]{4,3,2,1,0:T(8,128)(2,1)S(1)}, bf16[1,1,2,384,1024]{4,3,2,1,0:T(8,128)(2,1)}, u32[]{:S(2)}) copy-start(bf16[1,1,2,384,1024]{4,3,2,1,0:T(8,128)(2,1)} %param.2) | copy-start | bytes 4718596
  2.0 0.8 copy-start.1

commit v4 on v3

--- a/solution.py
+++ b/solution.py
@@ -14,7 +14,6 @@
 ROWS = 384
 COLS = 1024
 ITERS = 5
-EARLY = 4
 GROUPS = 8
 
 NX, NYH, NZ, NYL, NC = 4, 2, 8, 4, 2
@@ -29,6 +28,7 @@
 coef_a = 3.4445
 coef_b = -4.775
 coef_c = 2.0315
+FINAL_SCALE = 0.2 * math.sqrt(max(ROWS, COLS))
 
 bf16, f32 = jnp.bfloat16, jnp.float32
 
@@ -169,6 +169,11 @@
         sum_a[m] = total.astype(bf16)
         a2 += [send(sum_a.at[m, wrap(yh + t[0], NYH), :, cols_of(wrap(z + t[1], NZ))], got_a2.at[j, m], at_yz(t))
                for j, t in enumerate(yz_peers)]
+        if m == 0:
+            m4 = [send(m_b.at[:, x, yh], m_b.at[:, x, yh], at_xy(t)) for t in xy_peers]
+            m2.wait_recv()
+            m_a[:, :, :, own_cols] = m_pair[...]
+            m3 = [send(m_pair, m_a.at[:, :, :, own_cols], at_z(dz)) for dz in z_peers]
     for copy in b1:
         copy.wait_recv()
     total = own_b[...].astype(f32)
@@ -177,11 +182,6 @@
     sum_b[...] = total.astype(bf16)
     b2 = [send(sum_b.at[:, wrap(x + t[0], NX), wrap(yh + t[1], NYH)], got_b2.at[j], at_xy(t))
           for j, t in enumerate(xy_peers)]
-
-    m4 = [send(m_b.at[:, x, yh], m_b.at[:, x, yh], at_xy(t)) for t in xy_peers]
-    m2.wait_recv()
-    m_a[:, :, :, own_cols] = m_pair[...]
-    m3 = [send(m_pair, m_a.at[:, :, :, own_cols], at_z(dz)) for dz in z_peers]
 
     for copy in a2:
         copy.wait_recv()
@@ -213,7 +213,7 @@
             total = total + q_got[stage, j]
         return total
 
-    q = spread(0, z, z_peers, at_z)
+    q = spread(0, yh * NYL + yl, y_peers, at_y)
     all_a[:, yh, :, own_cols] = top.astype(bf16)
     all_b[:, x, yh] = rest.astype(bf16)
     here = all_a.at[:, yh, :, own_cols]
@@ -221,9 +221,9 @@
     here = all_b.at[:, x, yh]
     b3 = [send(here, here, at_xy(t)) for t in xy_peers]
     square = gather(0, q)
-    q = spread(1, x * NC + core, xc_peers, at_xc)
+    q = spread(1, z, z_peers, at_z)
     square = gather(1, q)
-    q = spread(2, yh * NYL + yl, y_peers, at_y)
+    q = spread(2, x * NC + core, xc_peers, at_xc)
     square = gather(2, q)
     square_sum = jnp.sum(jnp.sum(square, axis=1, keepdims=True), axis=0, keepdims=True)
     entries = GROUPS * MATS * ROWS * COLS
@@ -254,8 +254,9 @@
     for copy in a4[0] + b4[0]:
         copy.wait_recv()
     y0_ref[...] = normalized(x0_ref[...].reshape(ROWS, COLS))
-    for _ in range(EARLY):
+    for _ in range(ITERS - 1):
         y0_ref[...] = stepped(y0_ref[...]).astype(bf16)
+    y0_ref[...] = (stepped(y0_ref[...]) * FINAL_SCALE).astype(bf16)
 
     for copy in a4[1] + b4[1]:
         copy.wait_recv()
@@ -305,37 +306,23 @@
             pltpu.SemaphoreType.DMA((n_copies,)),
         ],
         compiler_params=pltpu.CompilerParams(
-            collective_id=0, has_side_effects=True, vmem_limit_bytes=32 << 20),
+            collective_id=0, has_side_effects=True, vmem_limit_bytes=52 << 20),
         cost_estimate=pl.CostEstimate(flops=2_900_000_000, bytes_accessed=8_000_000, transcendentals=0),
     )(partials, momentum)
 
 
-def newton_kernel(x1_ref, y0_ref, mi_ref, u_ref, mo_ref, cur, done, sem):
-    final_scale = 0.2 * math.sqrt(max(ROWS, COLS))
+def newton_kernel(x1_ref, y0_ref, mi_ref, u_ref, mo_ref, cur, sem):
+    first = pltpu.make_async_copy(y0_ref, u_ref.at[0], sem.at[0])
+    first.start()
     mo_ref[...] = mi_ref[...]
-    copies = []
-
-    def finish(m, value):
-        done[m] = (value * final_scale).astype(bf16)
-        copies.append(pltpu.make_async_copy(done.at[m], u_ref.at[m], sem.at[m]))
-        copies[-1].start()
-
-    cur[0] = y0_ref[...]
-    cur[1] = normalized(x1_ref[...].reshape(ROWS, COLS))
-    left = [ITERS - EARLY, ITERS]
-    for _ in range(ITERS):
-        work = [m for m in range(MATS) if left[m] > 0]
-        polys = {m: poly_of(cur[m]) for m in work}
-        for m in work:
-            here = cur[m]
-            value = coef_a * here.astype(f32) + jnp.dot(polys[m], here, preferred_element_type=f32)
-            left[m] -= 1
-            if left[m] > 0:
-                cur[m] = value.astype(bf16)
-            else:
-                finish(m, value)
-    for copy in copies:
-        copy.wait()
+    cur[...] = normalized(x1_ref[...].reshape(ROWS, COLS))
+    for _ in range(ITERS - 1):
+        cur[...] = stepped(cur[...]).astype(bf16)
+    cur[...] = (stepped(cur[...]) * FINAL_SCALE).astype(bf16)
+    second = pltpu.make_async_copy(cur, u_ref.at[1], sem.at[1])
+    second.start()
+    first.wait()
+    second.wait()
 
 
 def newton(x1, y0, momentum_out):
@@ -346,8 +333,7 @@
         out_shape=(jax.ShapeDtypeStruct((MATS, ROWS, COLS), bf16), jax.ShapeDtypeStruct((OWN, MATS, COLS), f32)),
         in_specs=[vmem, vmem, vmem],
         out_specs=(pl.BlockSpec(memory_space=pltpu.HBM), vmem),
-        scratch_shapes=[pltpu.VMEM((MATS, ROWS, COLS), bf16), pltpu.VMEM((MATS, ROWS, COLS), bf16),
-                        pltpu.SemaphoreType.DMA((MATS,))],
+        scratch_shapes=[pltpu.VMEM((ROWS, COLS), bf16), pltpu.SemaphoreType.DMA((MATS,))],
         compiler_params=pltpu.CompilerParams(vmem_limit_bytes=40 << 20),
         cost_estimate=pl.CostEstimate(flops=4_300_000_000, bytes_accessed=3_200_000, transcendentals=0),
     )(x1, y0, momentum_out)

time: 81.5 us -> 87.1 us (1.069)
  Pallas kernels: 77.9 us -> 85.4 us
  local copies, waits for them, and re-layouts: 2.2 us -> 0.79 us
    pallas_call x1, Pallas kernels: 69.3 us -> 77.6 us  [comm(): pl.pallas_call(comm_kernel, name='reduce_blend_gather', out_shape=(jax.Sh...]
    unnamed x4 -> x2, local copies, waits for them, and re-layouts: 2.2 us -> 0.79 us
where the time goes in v4:
time: 87.1 us; the launch traced here: 86.9 us
  Pallas kernels  85.4 us (98%)
    pallas_call x1, Pallas kernels, comm(): pl.pallas_call(comm_kernel, name='reduce_blend_gather', out_shape=(jax.Sh...  77.6 us
    pallas_call x1, Pallas kernels, newton(): pl.pallas_call(newton_kernel, name='newton_schulz', out_shape=(jax.ShapeD...  7.88 us

profile of v4, /device:TPU:1, one launch (start us, length us, event | category | flops | bytes accessed | tf_op | source)
XLA Modules:
  0.0 86.9 jit_solution(10116819689854977274)
XLA Ops:
  0.6 0.0 copy-start
  0.6 0.8 copy-done
  1.4 77.6 %reduce_blend_gather.1 = (bf16[4,2,48,1024]{3,2,1,0:T(8,128)(2,1)S(1)}, bf16[384,1024]{1,0:T(8,128)(2,1)S(1)}, f32[6,2,1024]{2,1,0:T(2,128)S(1)}) custom-call(bf16[2,4,2,48,1024]{4,3,2,1,0:T(8,128)(2,1)} %bitcast.9, f32[6,2,1024]{2,1,0:T(2,128)S(1)} %bitcast.8), custom_call_target="tpu_custom_call" | custom-call | flops 2900000000 | bytes 8000000 | tf_op jit(solution)/shard_map/reduce_blend_gather/pallas_call | solution.py:279
  79.0 7.9 %newton_schulz.1 = (bf16[2,384,1024]{2,1,0:T(8,128)(2,1)}, f32[6,2,1024]{2,1,0:T(2,128)}) custom-call(bf16[4,2,48,1024]{3,2,1,0:T(8,128)(2,1)S(1)} %get-tuple-element.7.x1_ref, bf16[384,1024]{1,0:T(8,128)(2,1)S(1)} %get-tuple-element.8.y0_ref, f32[6,2,1024]{2,1,0:T(2,128)S(1)} %get-tuple-element.9.mi_ref), custom_call_target="tpu_custom_call" | custom-call | flops 4300000256 | bytes 3200000 | tf_op jit(solution)/shard_map/newton_schulz/pallas_call | solution.py:330
Async XLA Ops:
  0.6 0.8 copy-start

commit v5 on v4

--- a/solution.py
+++ b/solution.py
@@ -14,6 +14,7 @@
 ROWS = 384
 COLS = 1024
 ITERS = 5
+PIECES = 2
 GROUPS = 8
 
 NX, NYH, NZ, NYL, NC = 4, 2, 8, 4, 2
@@ -59,10 +60,9 @@
     return coef_a * here.astype(f32) + jnp.dot(poly_of(here), here, preferred_element_type=f32)
 
 
-def comm_kernel(p_ref, m_ref, x1_ref, y0_ref, mo_ref, x0_ref, own_a, own_b, got_a, got_b, sum_a, sum_b, got_a2, got_b2,
-                all_a, all_b, m_out, m_got, m_pair, m_a, m_b, q_got, lsem, ssem, rsem):
+def comm_kernel(p_ref, m_ref, x1_ref, y0_ref, mo_ref, own_a, own_b, got_a, got_b, sum_a, sum_b, got_a2, got_b2,
+                s_all, m_all, m_out, m_got, q_got, lsem, ssem, rsem):
     x, yh, z, yl, core = place()
-    xs = (x0_ref, x1_ref)
     counter = [0]
 
     def wrap(v, n):
@@ -153,9 +153,20 @@
     for m in range(MATS):
         block = jnp.dot(pick, m_got[:, m].reshape(NZ * OWN_PAD, WIDE).astype(bf16),
                         preferred_element_type=f32).astype(bf16)
-        m_pair[m, yh] = block[0:TOP]
-        m_b[m, x, yh] = block[TOP:SLAB]
-    m2 = send(m_pair.at[:, yh], m_pair.at[:, yh], at_yz((1, 0)))
+        m_all[m, x, yh, :, own_cols] = block
+    here = m_all.at[:, x, yh, :, own_cols]
+    m2 = send(here, here, at_yz((1, 0)))
+
+    def hop(t, before):
+        for copy in before:
+            copy.wait_recv()
+        strip = m_all.at[:, x, :, :, cols_of(wrap(z + NZ - t + 1, NZ))]
+        copies = [send(strip, strip, at_z(1))]
+        if t < NZ // 2:
+            strip = m_all.at[:, x, :, :, cols_of(wrap(z + t - 1, NZ))]
+            copies.append(send(strip, strip, at_z(NZ - 1)))
+        return copies
+
 
     local_a.wait()
     local_b.wait()
@@ -169,11 +180,7 @@
         sum_a[m] = total.astype(bf16)
         a2 += [send(sum_a.at[m, wrap(yh + t[0], NYH), :, cols_of(wrap(z + t[1], NZ))], got_a2.at[j, m], at_yz(t))
                for j, t in enumerate(yz_peers)]
-        if m == 0:
-            m4 = [send(m_b.at[:, x, yh], m_b.at[:, x, yh], at_xy(t)) for t in xy_peers]
-            m2.wait_recv()
-            m_a[:, :, :, own_cols] = m_pair[...]
-            m3 = [send(m_pair, m_a.at[:, :, :, own_cols], at_z(dz)) for dz in z_peers]
+        hops = hop(1, [m2]) if m == 0 else hop(2, hops)
     for copy in b1:
         copy.wait_recv()
     total = own_b[...].astype(f32)
@@ -183,6 +190,12 @@
     b2 = [send(sum_b.at[:, wrap(x + t[0], NX), wrap(yh + t[1], NYH)], got_b2.at[j], at_xy(t))
           for j, t in enumerate(xy_peers)]
 
+    for t in range(3, NZ // 2 + 1):
+        hops = hop(t, hops)
+    for copy in hops:
+        copy.wait_recv()
+    m3 = [[send(m_all.at[m, x], m_all.at[m, x], at_x(dx)) for dx in x_peers] for m in range(MATS)]
+
     for copy in a2:
         copy.wait_recv()
     top = sum_a[:, yh, :, own_cols].astype(f32)
@@ -213,78 +226,67 @@
             total = total + q_got[stage, j]
         return total
 
-    q = spread(0, yh * NYL + yl, y_peers, at_y)
-    all_a[:, yh, :, own_cols] = top.astype(bf16)
-    all_b[:, x, yh] = rest.astype(bf16)
-    here = all_a.at[:, yh, :, own_cols]
-    a3 = [send(here, here, at_yz(t)) for t in yz_peers]
-    here = all_b.at[:, x, yh]
-    b3 = [send(here, here, at_xy(t)) for t in xy_peers]
+    q = spread(0, z, z_peers, at_z)
+    a3 = []
+    for m in range(MATS):
+        s_all[m, x, yh, 0:TOP, own_cols] = top[m].astype(bf16)
+        s_all[m, x, yh, TOP:SLAB, own_cols] = rest[m].astype(bf16)
+        here = s_all.at[m, x, yh, :, own_cols]
+        a3.append([send(here, here, at_yz(t)) for t in yz_peers])
+
+    def onward(m):
+        for copy in a3[m]:
+            copy.wait_recv()
+        strip = s_all.at[m, x]
+        return [send(strip, strip, at_x(dx)) for dx in x_peers]
+
     square = gather(0, q)
-    q = spread(1, z, z_peers, at_z)
+    q = spread(1, x * NC + core, xc_peers, at_xc)
+    a4 = [onward(0)]
     square = gather(1, q)
-    q = spread(2, x * NC + core, xc_peers, at_xc)
+    q = spread(2, yh * NYL + yl, y_peers, at_y)
+    a4.append(onward(1))
     square = gather(2, q)
     square_sum = jnp.sum(jnp.sum(square, axis=1, keepdims=True), axis=0, keepdims=True)
     entries = GROUPS * MATS * ROWS * COLS
     clip = jnp.minimum(1.0, math.sqrt(entries) / jnp.sqrt(square_sum + 1e-06))
     scale = (1.0 + decay_rate) * clip
 
-    for copy in m3 + a3:
-        copy.wait_recv()
-    a4 = []
-    b4 = []
-    for m in range(MATS):
-        for j in range(NYH):
-            xs[m][x, j, 0:TOP, :] = (
-                scale * all_a[m, j].astype(f32) + (decay_rate * decay_rate) * m_a[m, j].astype(f32)).astype(bf16)
-        strip = xs[m].at[x, :, 0:TOP, :]
-        a4.append([send(strip, strip, at_x(dx)) for dx in x_peers])
-        if m == 0:
-            for copy in m4 + b3:
-                copy.wait_recv()
-        for i in range(NX):
-            for j in range(NYH):
-                xs[m][i, j, TOP:SLAB, own_cols] = (
-                    scale * all_b[m, i, j].astype(f32)
-                    + (decay_rate * decay_rate) * m_b[m, i, j].astype(f32)).astype(bf16)
-        strip = xs[m].at[:, :, TOP:SLAB, own_cols]
-        b4.append([send(strip, strip, at_z(dz)) for dz in z_peers])
-
-    for copy in a4[0] + b4[0]:
-        copy.wait_recv()
-    y0_ref[...] = normalized(x0_ref[...].reshape(ROWS, COLS))
-    for _ in range(ITERS - 1):
-        y0_ref[...] = stepped(y0_ref[...]).astype(bf16)
-    y0_ref[...] = (stepped(y0_ref[...]) * FINAL_SCALE).astype(bf16)
-
-    for copy in a4[1] + b4[1]:
-        copy.wait_recv()
+    def blended(m):
+        for copy in m3[m] + a4[m]:
+            copy.wait_recv()
+        total = s_all[m].reshape(ROWS, COLS).astype(f32)
+        old = m_all[m].reshape(ROWS, COLS).astype(f32)
+        return (scale * total + (decay_rate * decay_rate) * old).astype(bf16)
 
     row = lax.broadcasted_iota(jnp.int32, (OWN_PAD, SLAB), 0)
     col = lax.broadcasted_iota(jnp.int32, (OWN_PAD, SLAB), 1)
     pick = ((col == z * OWN + row) & (row < OWN)).astype(f32).astype(bf16)
     for m in range(MATS):
-        mine = jnp.dot(pick, xs[m][x, yh], preferred_element_type=f32)[0:OWN]
-        old = m_ref[:, m, :]
-        grad = (mine - (decay_rate * decay_rate) * old) * (1.0 / (1.0 + decay_rate))
-        mo_ref[:, m, :] = decay_rate * old + grad
+        mine = jnp.dot(pick, s_all[m, x, yh], preferred_element_type=f32)[0:OWN]
+        mo_ref[:, m, :] = decay_rate * m_ref[:, m, :] + clip * mine
+
+    y0_ref[...] = normalized(blended(0))
+    for _ in range(ITERS - 2):
+        y0_ref[...] = stepped(y0_ref[...]).astype(bf16)
+    x1_ref[...] = normalized(blended(1))
+    y0_ref[...] = stepped(y0_ref[...]).astype(bf16)
+    y0_ref[...] = (stepped(y0_ref[...]) * FINAL_SCALE).astype(bf16)
     for copy in sent:
         copy.wait_send()
 
 
 def comm(partials, momentum):
     z_n, yz_n, xy_n = NZ - 1, NYH * NZ - 1, NX * NYH - 1
-    n_copies = 4 * (NX - 1) + 3 * z_n + 3 * yz_n + 2 * xy_n + 2 * z_n + xy_n + 1 + z_n + (NX * NC - 1) + (NYH * NYL - 1)
+    n_copies = 6 * (NX - 1) + 3 * z_n + 1 + 4 * yz_n + xy_n + z_n + (NX * NC - 1) + (NYH * NYL - 1)
     return pl.pallas_call(
         comm_kernel,
         name="reduce_blend_gather",
-        out_shape=(jax.ShapeDtypeStruct((NX, NYH, SLAB, COLS), bf16), jax.ShapeDtypeStruct((ROWS, COLS), bf16),
+        out_shape=(jax.ShapeDtypeStruct((ROWS, COLS), bf16), jax.ShapeDtypeStruct((ROWS, COLS), bf16),
                    jax.ShapeDtypeStruct((OWN, MATS, COLS), f32)),
         in_specs=[pl.BlockSpec(memory_space=pltpu.HBM), pl.BlockSpec(memory_space=pltpu.VMEM)],
         out_specs=(pl.BlockSpec(memory_space=pltpu.VMEM),) * 3,
         scratch_shapes=[
-            pltpu.VMEM((NX, NYH, SLAB, COLS), bf16),
             pltpu.VMEM((MATS, NYH, TOP, COLS), bf16),
             pltpu.VMEM((MATS, NX, NYH, REST, WIDE), bf16),
             pltpu.VMEM((MATS, NX - 1, NYH, TOP, COLS), bf16),
@@ -293,13 +295,10 @@
             pltpu.VMEM((MATS, NX, NYH, REST, WIDE), bf16),
             pltpu.VMEM((NYH * NZ - 1, MATS, TOP, WIDE), bf16),
             pltpu.VMEM((NX * NYH - 1, MATS, REST, WIDE), bf16),
-            pltpu.VMEM((MATS, NYH, TOP, COLS), bf16),
-            pltpu.VMEM((MATS, NX, NYH, REST, WIDE), bf16),
+            pltpu.VMEM((MATS, NX, NYH, SLAB, COLS), bf16),
+            pltpu.VMEM((MATS, NX, NYH, SLAB, COLS), bf16),
             pltpu.VMEM((MATS, OWN_PAD, COLS), f32),
             pltpu.VMEM((NZ, MATS, OWN_PAD, WIDE), f32),
-            pltpu.VMEM((MATS, NYH, TOP, WIDE), bf16),
-            pltpu.VMEM((MATS, NYH, TOP, COLS), bf16),
-            pltpu.VMEM((MATS, NX, NYH, REST, WIDE), bf16),
             pltpu.VMEM((3, 8, 8, WIDE), f32),
             pltpu.SemaphoreType.DMA((2,)),
             pltpu.SemaphoreType.DMA((n_copies,)),
@@ -312,17 +311,22 @@
 
 
 def newton_kernel(x1_ref, y0_ref, mi_ref, u_ref, mo_ref, cur, sem):
-    first = pltpu.make_async_copy(y0_ref, u_ref.at[0], sem.at[0])
-    first.start()
+    copies = [pltpu.make_async_copy(y0_ref, u_ref.at[0], sem.at[0])]
+    copies[0].start()
     mo_ref[...] = mi_ref[...]
-    cur[...] = normalized(x1_ref[...].reshape(ROWS, COLS))
+    here = x1_ref[...]
     for _ in range(ITERS - 1):
-        cur[...] = stepped(cur[...]).astype(bf16)
-    cur[...] = (stepped(cur[...]) * FINAL_SCALE).astype(bf16)
-    second = pltpu.make_async_copy(cur, u_ref.at[1], sem.at[1])
-    second.start()
-    first.wait()
-    second.wait()
+        here = stepped(here).astype(bf16)
+    poly = poly_of(here)
+    for i in range(PIECES):
+        cols = slice(i * COLS // PIECES, (i + 1) * COLS // PIECES)
+        part = here[:, cols]
+        last = coef_a * part.astype(f32) + jnp.dot(poly, part, preferred_element_type=f32)
+        cur[:, cols] = (last * FINAL_SCALE).astype(bf16)
+        copies.append(pltpu.make_async_copy(cur.at[:, cols], u_ref.at[1, :, cols], sem.at[1 + i]))
+        copies[-1].start()
+    for copy in copies:
+        copy.wait()
 
 
 def newton(x1, y0, momentum_out):
@@ -333,7 +337,7 @@
         out_shape=(jax.ShapeDtypeStruct((MATS, ROWS, COLS), bf16), jax.ShapeDtypeStruct((OWN, MATS, COLS), f32)),
         in_specs=[vmem, vmem, vmem],
         out_specs=(pl.BlockSpec(memory_space=pltpu.HBM), vmem),
-        scratch_shapes=[pltpu.VMEM((ROWS, COLS), bf16), pltpu.SemaphoreType.DMA((MATS,))],
+        scratch_shapes=[pltpu.VMEM((ROWS, COLS), bf16), pltpu.SemaphoreType.DMA((1 + PIECES,))],
         compiler_params=pltpu.CompilerParams(vmem_limit_bytes=40 << 20),
         cost_estimate=pl.CostEstimate(flops=4_300_000_000, bytes_accessed=3_200_000, transcendentals=0),
     )(x1, y0, momentum_out)

time: 87.1 us -> 94.2 us (1.082)
  Pallas kernels: 85.4 us -> 92.5 us
    pallas_call x1, Pallas kernels: 77.6 us -> 85.1 us  [comm(): pl.pallas_call(comm_kernel, name='reduce_blend_gather', out_shape=(jax.Sh...]
where the time goes in v5:
time: 94.2 us; the launch traced here: 94 us
  Pallas kernels  92.5 us (98%)
    pallas_call x1, Pallas kernels, comm(): pl.pallas_call(comm_kernel, name='reduce_blend_gather', out_shape=(jax.Sh...  85.1 us
    pallas_call x1, Pallas kernels, newton(): pl.pallas_call(newton_kernel, name='newton_schulz', out_shape=(jax.ShapeD...  7.45 us

profile of v5, /device:TPU:1, one launch (start us, length us, event | category | flops | bytes accessed | tf_op | source)
XLA Modules:
  0.0 94.0 jit_solution(16292576462109119719)
XLA Ops:
  0.6 0.0 copy-start
  0.6 0.8 copy-done
  1.4 85.1 %reduce_blend_gather.1 = (bf16[384,1024]{1,0:T(8,128)(2,1)S(1)}, bf16[384,1024]{1,0:T(8,128)(2,1)S(1)}, f32[6,2,1024]{2,1,0:T(2,128)S(1)}) custom-call(bf16[2,4,2,48,1024]{4,3,2,1,0:T(8,128)(2,1)} %bitcast.9, f32[6,2,1024]{2,1,0:T(2,128)S(1)} %bitcast.8), custom_call_target="tpu_custom_call" | custom-call | flops 2900000000 | bytes 8000000 | tf_op jit(solution)/shard_map/reduce_blend_gather/pallas_call | solution.py:282
  86.5 7.4 %newton_schulz.1 = (bf16[2,384,1024]{2,1,0:T(8,128)(2,1)}, f32[6,2,1024]{2,1,0:T(2,128)}) custom-call(bf16[384,1024]{1,0:T(8,128)(2,1)S(1)} %get-tuple-element.7.x1_ref, bf16[384,1024]{1,0:T(8,128)(2,1)S(1)} %get-tuple-element.8.y0_ref, f32[6,2,1024]{2,1,0:T(2,128)S(1)} %get-tuple-element.9.mi_ref), custom_call_target="tpu_custom_call" | custom-call | flops 4300000256 | bytes 3200000 | tf_op jit(solution)/shard_map/newton_schulz/pallas_call | solution.py:334
Async XLA Ops:
  0.6 0.8 copy-start

commit v6 on v4

--- a/solution.py
+++ b/solution.py
@@ -14,6 +14,7 @@
 ROWS = 384
 COLS = 1024
 ITERS = 5
+PIECES = 2
 GROUPS = 8
 
 NX, NYH, NZ, NYL, NC = 4, 2, 8, 4, 2
@@ -169,11 +170,6 @@
         sum_a[m] = total.astype(bf16)
         a2 += [send(sum_a.at[m, wrap(yh + t[0], NYH), :, cols_of(wrap(z + t[1], NZ))], got_a2.at[j, m], at_yz(t))
                for j, t in enumerate(yz_peers)]
-        if m == 0:
-            m4 = [send(m_b.at[:, x, yh], m_b.at[:, x, yh], at_xy(t)) for t in xy_peers]
-            m2.wait_recv()
-            m_a[:, :, :, own_cols] = m_pair[...]
-            m3 = [send(m_pair, m_a.at[:, :, :, own_cols], at_z(dz)) for dz in z_peers]
     for copy in b1:
         copy.wait_recv()
     total = own_b[...].astype(f32)
@@ -183,11 +179,28 @@
     b2 = [send(sum_b.at[:, wrap(x + t[0], NX), wrap(yh + t[1], NYH)], got_b2.at[j], at_xy(t))
           for j, t in enumerate(xy_peers)]
 
+    m4 = [send(m_b.at[:, x, yh], m_b.at[:, x, yh], at_xy(t)) for t in xy_peers]
+    m2.wait_recv()
+    m_a[:, :, :, own_cols] = m_pair[...]
+
+    def hop(t, before):
+        for copy in before:
+            copy.wait_recv()
+        copies = []
+        p = m_a.at[:, :, :, cols_of(wrap(z + NZ - t + 1, NZ))]
+        copies.append(send(p, p, at_z(1)))
+        if t < NZ // 2:
+            n = m_a.at[:, :, :, cols_of(wrap(z + t - 1, NZ))]
+            copies.append(send(n, n, at_z(NZ - 1)))
+        return copies
+
+    h1 = hop(1, [])
     for copy in a2:
         copy.wait_recv()
     top = sum_a[:, yh, :, own_cols].astype(f32)
     for j in range(len(yz_peers)):
         top = top + got_a2[j].astype(f32)
+    h2 = hop(2, h1)
     for copy in b2:
         copy.wait_recv()
     rest = sum_b[:, x, yh].astype(f32)
@@ -213,17 +226,23 @@
             total = total + q_got[stage, j]
         return total
 
-    q = spread(0, yh * NYL + yl, y_peers, at_y)
+    q = spread(0, z, z_peers, at_z)
     all_a[:, yh, :, own_cols] = top.astype(bf16)
     all_b[:, x, yh] = rest.astype(bf16)
     here = all_a.at[:, yh, :, own_cols]
-    a3 = [send(here, here, at_yz(t)) for t in yz_peers]
+    pair = send(here, here, at_yz((1, 0)))
     here = all_b.at[:, x, yh]
     b3 = [send(here, here, at_xy(t)) for t in xy_peers]
+    h3 = hop(3, h2)
     square = gather(0, q)
-    q = spread(1, z, z_peers, at_z)
+    q = spread(1, x * NC + core, xc_peers, at_xc)
+    pair.wait_recv()
+    here = all_a.at[:, :, :, own_cols]
+    a3 = [send(here, here, at_z(dz)) for dz in z_peers]
     square = gather(1, q)
-    q = spread(2, x * NC + core, xc_peers, at_xc)
+    q = spread(2, yh * NYL + yl, y_peers, at_y)
+    h4 = hop(4, h3)
+    m3 = h4
     square = gather(2, q)
     square_sum = jnp.sum(jnp.sum(square, axis=1, keepdims=True), axis=0, keepdims=True)
     entries = GROUPS * MATS * ROWS * COLS
@@ -312,17 +331,22 @@
 
 
 def newton_kernel(x1_ref, y0_ref, mi_ref, u_ref, mo_ref, cur, sem):
-    first = pltpu.make_async_copy(y0_ref, u_ref.at[0], sem.at[0])
-    first.start()
+    copies = [pltpu.make_async_copy(y0_ref, u_ref.at[0], sem.at[0])]
+    copies[0].start()
     mo_ref[...] = mi_ref[...]
-    cur[...] = normalized(x1_ref[...].reshape(ROWS, COLS))
+    here = normalized(x1_ref[...].reshape(ROWS, COLS))
     for _ in range(ITERS - 1):
-        cur[...] = stepped(cur[...]).astype(bf16)
-    cur[...] = (stepped(cur[...]) * FINAL_SCALE).astype(bf16)
-    second = pltpu.make_async_copy(cur, u_ref.at[1], sem.at[1])
-    second.start()
-    first.wait()
-    second.wait()
+        here = stepped(here).astype(bf16)
+    poly = poly_of(here)
+    for i in range(PIECES):
+        cols = slice(i * COLS // PIECES, (i + 1) * COLS // PIECES)
+        part = here[:, cols]
+        last = coef_a * part.astype(f32) + jnp.dot(poly, part, preferred_element_type=f32)
+        cur[:, cols] = (last * FINAL_SCALE).astype(bf16)
+        copies.append(pltpu.make_async_copy(cur.at[:, cols], u_ref.at[1, :, cols], sem.at[1 + i]))
+        copies[-1].start()
+    for copy in copies:
+        copy.wait()
 
 
 def newton(x1, y0, momentum_out):
@@ -333,7 +357,7 @@
         out_shape=(jax.ShapeDtypeStruct((MATS, ROWS, COLS), bf16), jax.ShapeDtypeStruct((OWN, MATS, COLS), f32)),
         in_specs=[vmem, vmem, vmem],
         out_specs=(pl.BlockSpec(memory_space=pltpu.HBM), vmem),
-        scratch_shapes=[pltpu.VMEM((ROWS, COLS), bf16), pltpu.SemaphoreType.DMA((MATS,))],
+        scratch_shapes=[pltpu.VMEM((ROWS, COLS), bf16), pltpu.SemaphoreType.DMA((1 + PIECES,))],
         compiler_params=pltpu.CompilerParams(vmem_limit_bytes=40 << 20),
         cost_estimate=pl.CostEstimate(flops=4_300_000_000, bytes_accessed=3_200_000, transcendentals=0),
     )(x1, y0, momentum_out)

time: 87.1 us -> 79.3 us (0.910); the launches traced: 86.9 us -> 77.9 us
  Pallas kernels: 85.4 us -> 76.4 us
    pallas_call x1, Pallas kernels: 77.6 us -> 68.7 us  [comm(): pl.pallas_call(comm_kernel, name='reduce_blend_gather', out_shape=(jax.Sh...]
where the time goes in v6:
time: 79.3 us; the launch traced here: 77.9 us
  Pallas kernels  76.4 us (96%)
    pallas_call x1, Pallas kernels, comm(): pl.pallas_call(comm_kernel, name='reduce_blend_gather', out_shape=(jax.Sh...  68.7 us
    pallas_call x1, Pallas kernels, newton(): pl.pallas_call(newton_kernel, name='newton_schulz', out_shape=(jax.ShapeD...  7.69 us

profile of v6, /device:TPU:1, one launch (start us, length us, event | category | flops | bytes accessed | tf_op | source)
XLA Modules:
  0.0 77.9 jit_solution(11467717608254000682)
XLA Ops:
  0.6 0.0 copy-start
  0.6 0.8 %copy-done = f32[1,2,6,1024]{3,1,2,0:T(2,128)S(1)} copy-done((f32[1,2,6,1024]{3,1,2,0:T(2,128)S(1)}, f32[1,2,6,1024]{3,1,2,0:T(2,128)}, u32[]{:S(2)}) %copy-start) | copy-done | bytes 49176
  1.4 68.7 %reduce_blend_gather.1 = (bf16[4,2,48,1024]{3,2,1,0:T(8,128)(2,1)S(1)}, bf16[384,1024]{1,0:T(8,128)(2,1)S(1)}, f32[6,2,1024]{2,1,0:T(2,128)S(1)}) custom-call(bf16[2,4,2,48,1024]{4,3,2,1,0:T(8,128)(2,1)} %bitcast.9, f32[6,2,1024]{2,1,0:T(2,128)S(1)} %bitcast.8), custom_call_target="tpu_custom_call" | custom-call | flops 2900000000 | bytes 8000000 | tf_op jit(solution)/shard_map/reduce_blend_gather/pallas_call | solution.py:298
  70.2 7.7 %newton_schulz.1 = (bf16[2,384,1024]{2,1,0:T(8,128)(2,1)}, f32[6,2,1024]{2,1,0:T(2,128)}) custom-call(bf16[4,2,48,1024]{3,2,1,0:T(8,128)(2,1)S(1)} %get-tuple-element.7.x1_ref, bf16[384,1024]{1,0:T(8,128)(2,1)S(1)} %get-tuple-element.8.y0_ref, f32[6,2,1024]{2,1,0:T(2,128)S(1)} %get-tuple-element.9.mi_ref), custom_call_target="tpu_custom_call" | custom-call | flops 4300000256 | bytes 3200000 | tf_op jit(solution)/shard_map/newton_schulz/pallas_call | solution.py:354
Async XLA Ops:
  0.6 0.8 %copy-start = (f32[1,2,6,1024]{3,1,2,0:T(2,128)S(1)}, f32[1,2,6,1024]{3,1,2,0:T(2,128)}, u32[]{:S(2)}) copy-start(f32[1,2,6,1024]{3,1,2,0:T(2,128)} %param.3) | copy-start | bytes 147460

commit v7 on v6

--- a/solution.py
+++ b/solution.py
@@ -81,7 +81,7 @@
         sent.append(copy)
         return copy
 
-    x_peers = list(range(1, NX))
+    x_peers = sorted(range(1, NX), key=lambda d: -min(d, NX - d))
     z_peers = sorted(range(1, NZ), key=lambda d: -min(d, NZ - d))
     y_peers = list(range(1, NYH * NYL))
     yz_peers = [(dy, dz) for dy in range(NYH) for dz in range(NZ) if (dy, dz) != (0, 0)][::-1]
@@ -249,19 +249,11 @@
     clip = jnp.minimum(1.0, math.sqrt(entries) / jnp.sqrt(square_sum + 1e-06))
     scale = (1.0 + decay_rate) * clip
 
-    for copy in m3 + a3:
+    for copy in m4 + b3:
         copy.wait_recv()
     a4 = []
     b4 = []
     for m in range(MATS):
-        for j in range(NYH):
-            xs[m][x, j, 0:TOP, :] = (
-                scale * all_a[m, j].astype(f32) + (decay_rate * decay_rate) * m_a[m, j].astype(f32)).astype(bf16)
-        strip = xs[m].at[x, :, 0:TOP, :]
-        a4.append([send(strip, strip, at_x(dx)) for dx in x_peers])
-        if m == 0:
-            for copy in m4 + b3:
-                copy.wait_recv()
         for i in range(NX):
             for j in range(NYH):
                 xs[m][i, j, TOP:SLAB, own_cols] = (
@@ -269,6 +261,14 @@
                     + (decay_rate * decay_rate) * m_b[m, i, j].astype(f32)).astype(bf16)
         strip = xs[m].at[:, :, TOP:SLAB, own_cols]
         b4.append([send(strip, strip, at_z(dz)) for dz in z_peers])
+        if m == 0:
+            for copy in m3 + a3:
+                copy.wait_recv()
+        for j in range(NYH):
+            xs[m][x, j, 0:TOP, :] = (
+                scale * all_a[m, j].astype(f32) + (decay_rate * decay_rate) * m_a[m, j].astype(f32)).astype(bf16)
+        strip = xs[m].at[x, :, 0:TOP, :]
+        a4.append([send(strip, strip, at_x(dx)) for dx in x_peers])
 
     for copy in a4[0] + b4[0]:
         copy.wait_recv()

time: 79.3 us -> 80.1 us (1.010); the launches traced: 77.9 us -> 79.5 us
  Pallas kernels: 76.4 us -> 78.1 us
    pallas_call x1, Pallas kernels: 68.7 us -> 70.4 us  [comm(): pl.pallas_call(comm_kernel, name='reduce_blend_gather', out_shape=(jax.Sh...]
where the time goes in v7:
time: 80.1 us; the launch traced here: 79.5 us
  Pallas kernels  78.1 us (98%)
    pallas_call x1, Pallas kernels, comm(): pl.pallas_call(comm_kernel, name='reduce_blend_gather', out_shape=(jax.Sh...  70.4 us
    pallas_call x1, Pallas kernels, newton(): pl.pallas_call(newton_kernel, name='newton_schulz', out_shape=(jax.ShapeD...  7.68 us

profile of v7, /device:TPU:1, one launch (start us, length us, event | category | flops | bytes accessed | tf_op | source)
XLA Modules:
  0.0 79.5 jit_solution(1237211635082575718)
XLA Ops:
  0.6 0.0 copy-start
  0.6 0.8 copy-done
  1.4 70.4 %reduce_blend_gather.1 = (bf16[4,2,48,1024]{3,2,1,0:T(8,128)(2,1)S(1)}, bf16[384,1024]{1,0:T(8,128)(2,1)S(1)}, f32[6,2,1024]{2,1,0:T(2,128)S(1)}) custom-call(bf16[2,4,2,48,1024]{4,3,2,1,0:T(8,128)(2,1)} %bitcast.9, f32[6,2,1024]{2,1,0:T(2,128)S(1)} %bitcast.8), custom_call_target="tpu_custom_call" | custom-call | flops 2900000000 | bytes 8000000 | tf_op jit(solution)/shard_map/reduce_blend_gather/pallas_call | solution.py:298
  71.9 7.7 %newton_schulz.1 = (bf16[2,384,1024]{2,1,0:T(8,128)(2,1)}, f32[6,2,1024]{2,1,0:T(2,128)}) custom-call(bf16[4,2,48,1024]{3,2,1,0:T(8,128)(2,1)S(1)} %get-tuple-element.7.x1_ref, bf16[384,1024]{1,0:T(8,128)(2,1)S(1)} %get-tuple-element.8.y0_ref, f32[6,2,1024]{2,1,0:T(2,128)S(1)} %get-tuple-element.9.mi_ref), custom_call_target="tpu_custom_call" | custom-call | flops 4300000256 | bytes 3200000 | tf_op jit(solution)/shard_map/newton_schulz/pallas_call | solution.py:354
Async XLA Ops:
  0.6 0.8 %copy-start = (f32[1,2,6,1024]{3,1,2,0:T(2,128)S(1)}, f32[1,2,6,1024]{3,1,2,0:T(2,128)}, u32[]{:S(2)}) copy-start(f32[1,2,6,1024]{3,1,2,0:T(2,128)} %param.3) | copy-start | bytes 147460

commit v8 on v6

--- a/solution.py
+++ b/solution.py
@@ -14,6 +14,7 @@
 ROWS = 384
 COLS = 1024
 ITERS = 5
+EARLY = 3
 PIECES = 2
 GROUPS = 8
 
@@ -273,9 +274,8 @@
     for copy in a4[0] + b4[0]:
         copy.wait_recv()
     y0_ref[...] = normalized(x0_ref[...].reshape(ROWS, COLS))
-    for _ in range(ITERS - 1):
+    for _ in range(EARLY):
         y0_ref[...] = stepped(y0_ref[...]).astype(bf16)
-    y0_ref[...] = (stepped(y0_ref[...]) * FINAL_SCALE).astype(bf16)
 
     for copy in a4[1] + b4[1]:
         copy.wait_recv()
@@ -330,21 +330,55 @@
     )(partials, momentum)
 
 
-def newton_kernel(x1_ref, y0_ref, mi_ref, u_ref, mo_ref, cur, sem):
-    copies = [pltpu.make_async_copy(y0_ref, u_ref.at[0], sem.at[0])]
-    copies[0].start()
+def poly_by_halves(here, out):
+    half = 256
+    left = lax.dot_general(here, here[0:half], (((1,), (1,)), ((), ())), preferred_element_type=f32)
+    corner = lax.dot_general(here[half:], here[half:], (((1,), (1,)), ((), ())), preferred_element_type=f32)
+    for last in (False, True):
+        out[:, 0:half] = left.astype(bf16)
+        out[half:, half:] = corner.astype(bf16)
+        out[0:half, half:] = left[half:].T.astype(bf16)
+        gram = out[...]
+        if last:
+            return gram
+        left = coef_b * gram[:, 0:half].astype(f32) + coef_c * jnp.dot(
+            gram, gram[:, 0:half], preferred_element_type=f32)
+        corner = coef_b * gram[half:, half:].astype(f32) + coef_c * jnp.dot(
+            gram[half:], gram[:, half:], preferred_element_type=f32)
+
+
+def newton_kernel(x1_ref, y0_ref, mi_ref, u_ref, mo_ref, cur, poly_buf, sem):
     mo_ref[...] = mi_ref[...]
-    here = normalized(x1_ref[...].reshape(ROWS, COLS))
-    for _ in range(ITERS - 1):
-        here = stepped(here).astype(bf16)
+    copies = []
+
+    def write(m, i, cols, value):
+        cur[m, :, cols] = (value * FINAL_SCALE).astype(bf16)
+        copies.append(pltpu.make_async_copy(cur.at[m, :, cols], u_ref.at[m, :, cols], sem.at[i]))
+        copies[-1].start()
+
+    def advance(m, poly):
+        here = cur[m]
+        return coef_a * here.astype(f32) + jnp.dot(poly, here, preferred_element_type=f32)
+
+    cur[0] = y0_ref[...]
+    cur[1] = normalized(x1_ref[...].reshape(ROWS, COLS))
+    pairs = ITERS - EARLY
+    for t in range(pairs):
+        polys = [poly_by_halves(cur[m], poly_buf.at[m]) for m in range(MATS)]
+        value = advance(0, polys[0])
+        if t + 1 < pairs:
+            cur[0] = value.astype(bf16)
+        else:
+            write(0, 0, slice(0, COLS), value)
+        cur[1] = advance(1, polys[1]).astype(bf16)
+    for _ in range(ITERS - 1 - pairs):
+        cur[1] = stepped(cur[1]).astype(bf16)
+    here = cur[1]
     poly = poly_of(here)
     for i in range(PIECES):
         cols = slice(i * COLS // PIECES, (i + 1) * COLS // PIECES)
         part = here[:, cols]
-        last = coef_a * part.astype(f32) + jnp.dot(poly, part, preferred_element_type=f32)
-        cur[:, cols] = (last * FINAL_SCALE).astype(bf16)
-        copies.append(pltpu.make_async_copy(cur.at[:, cols], u_ref.at[1, :, cols], sem.at[1 + i]))
-        copies[-1].start()
+        write(1, 1 + i, cols, coef_a * part.astype(f32) + jnp.dot(poly, part, preferred_element_type=f32))
     for copy in copies:
         copy.wait()
 
@@ -357,7 +391,8 @@
         out_shape=(jax.ShapeDtypeStruct((MATS, ROWS, COLS), bf16), jax.ShapeDtypeStruct((OWN, MATS, COLS), f32)),
         in_specs=[vmem, vmem, vmem],
         out_specs=(pl.BlockSpec(memory_space=pltpu.HBM), vmem),
-        scratch_shapes=[pltpu.VMEM((ROWS, COLS), bf16), pltpu.SemaphoreType.DMA((1 + PIECES,))],
+        scratch_shapes=[pltpu.VMEM((MATS, ROWS, COLS), bf16), pltpu.VMEM((MATS, ROWS, ROWS), bf16),
+                        pltpu.SemaphoreType.DMA((1 + PIECES,))],
         compiler_params=pltpu.CompilerParams(vmem_limit_bytes=40 << 20),
         cost_estimate=pl.CostEstimate(flops=4_300_000_000, bytes_accessed=3_200_000, transcendentals=0),
     )(x1, y0, momentum_out)

time: 79.3 us -> 78.7 us (level); the launches traced: 77.9 us -> 78.5 us
    pallas_call x1, Pallas kernels: 7.69 us -> 9.25 us  [newton(): pl.pallas_call(newton_kernel, name='newton_schulz', out_shape=(jax.ShapeD...]
    pallas_call x1, Pallas kernels: 68.7 us -> 67.8 us  [comm(): pl.pallas_call(comm_kernel, name='reduce_blend_gather', out_shape=(jax.Sh...]
where the time goes in v8:
time: 78.7 us; the launch traced here: 78.5 us
  Pallas kernels  77 us (98%)
  local copies, waits for them, and re-layouts  0.79 us (1%)
    pallas_call x1, Pallas kernels, comm(): pl.pallas_call(comm_kernel, name='reduce_blend_gather', out_shape=(jax.Sh...  67.8 us
    pallas_call x1, Pallas kernels, newton(): pl.pallas_call(newton_kernel, name='newton_schulz', out_shape=(jax.ShapeD...  9.25 us

profile of v8, /device:TPU:1, one launch (start us, length us, event | category | flops | bytes accessed | tf_op | source)
XLA Modules:
  0.0 78.5 jit_solution(11238521774258207263)
XLA Ops:
  0.6 0.0 copy-start
  0.6 0.8 %copy-done = f32[1,2,6,1024]{3,1,2,0:T(2,128)S(1)} copy-done((f32[1,2,6,1024]{3,1,2,0:T(2,128)S(1)}, f32[1,2,6,1024]{3,1,2,0:T(2,128)}, u32[]{:S(2)}) %copy-start) | copy-done | bytes 49176
  1.4 67.8 %reduce_blend_gather.1 = (bf16[4,2,48,1024]{3,2,1,0:T(8,128)(2,1)S(1)}, bf16[384,1024]{1,0:T(8,128)(2,1)S(1)}, f32[6,2,1024]{2,1,0:T(2,128)S(1)}) custom-call(bf16[2,4,2,48,1024]{4,3,2,1,0:T(8,128)(2,1)} %bitcast.9, f32[6,2,1024]{2,1,0:T(2,128)S(1)} %bitcast.8), custom_call_target="tpu_custom_call" | custom-call | flops 2900000000 | bytes 8000000 | tf_op jit(solution)/shard_map/reduce_blend_gather/pallas_call | solution.py:298
  69.2 9.3 %newton_schulz.1 = (bf16[2,384,1024]{2,1,0:T(8,128)(2,1)}, f32[6,2,1024]{2,1,0:T(2,128)}) custom-call(bf16[4,2,48,1024]{3,2,1,0:T(8,128)(2,1)S(1)} %get-tuple-element.7.x1_ref, bf16[384,1024]{1,0:T(8,128)(2,1)S(1)} %get-tuple-element.8.y0_ref, f32[6,2,1024]{2,1,0:T(2,128)S(1)} %get-tuple-element.9.mi_ref), custom_call_target="tpu_custom_call" | custom-call | flops 4300000256 | bytes 3200000 | tf_op jit(solution)/shard_map/newton_schulz/pallas_call | solution.py:388
Async XLA Ops:
  0.6 0.8 %copy-start = (f32[1,2,6,1024]{3,1,2,0:T(2,128)S(1)}, f32[1,2,6,1024]{3,1,2,0:T(2,128)}, u32[]{:S(2)}) copy-start(f32[1,2,6,1024]{3,1,2,0:T(2,128)} %param.3) | copy-start | bytes 147460
